TPU v7x, 32 devices: a whole 2x2x4 slice. The times are simulated.
32 devices in a mesh: seq: 8 (over z, core), ch: 2 (over y), win: 2 (over x).
Axes of the slice: x: 2, y: 2, z: 4, core: 2. Of those that a mesh axis runs over, the one named last changes fastest.
Arguments:
- inputs: bfloat16 [8, 768, 24576], P('win', 'ch', 'seq')
- lengths: int32 [8], P('win'), may hold values from 6144 to 24576, as said below
- gain_in: float32 [768], P('ch'), may hold values from 0.1 to 1.9
- offset_in: float32 [768], P('ch'), may hold values from -3 to 3
- conv_weight: bfloat16 [3, 768, 384], P(None, 'ch'), may hold values from -0.125 to 0.125
- gain_mid: float32 [384], replicated, may hold values from 0.1 to 1.9
- offset_mid: float32 [384], replicated, may hold values from -3 to 3
- point_weight: bfloat16 [384, 768], P(None, 'ch'), may hold values from -0.625 to 0.625
- point_bias: float32 [768], P('ch'), may hold values from -3 to 3
- cotangent: bfloat16 [8, 768, 24576], P('win', 'ch', 'seq'), may hold values from -6 to 6
Outputs:
- outputs: bfloat16 [8, 768, 24576], P('win', 'ch', 'seq')
- grad_inputs: bfloat16 [8, 768, 24576], P('win', 'ch', 'seq')
- grad_gain_in: float32 [768], P('ch')
- grad_offset_in: float32 [768], P('ch')
- grad_conv: float32 [3, 768, 384], P(None, 'ch')
- grad_gain_mid: float32 [384], P('ch')
- grad_offset_mid: float32 [384], P('ch')
- grad_point: float32 [384, 768], P(None, 'ch')
- grad_bias: float32 [768], P('ch')
Inputs may be any that keep to these rules, and one draw needn't show every extreme that they name: `lengths`: among the 4 windows of each index of win, one has all 24576 bins valid and another a quarter of them.
All inputs are finite; a program needn't handle non-finite values.
Results may differ from a plain program's by a relative error of at most 0.0068.
Values may be sent and summed in bfloat16 or wider, within the bound.
A program may use at most 256 MiB of HBM per device.

v0:
```python
import jax
import jax.numpy as jnp
from jax import lax
from jax.sharding import PartitionSpec as P

DILATION_BINS = 57


EPS = 1e-05


def with_halo(cells, sides, width):
    for axis, dim in sides:
        count = lax.axis_size(axis)
        ends = count - 1
        head = lax.slice_in_dim(cells, 0, width, axis=dim)
        tail = lax.slice_in_dim(cells, cells.shape[dim] - width, cells.shape[dim], axis=dim)
        cells = jnp.concatenate(
            [
                lax.ppermute(tail, axis, [(i, (i + 1) % count) for i in range(ends)]),
                cells,
                lax.ppermute(head, axis, [((i + 1) % count, i) for i in range(ends)]),
            ],
            axis=dim,
        )
    return cells


def norm_sums(first_term, second_term):
    return lax.psum((first_term, second_term), ("seq", "win"))


def column(vector):
    return vector[:, None]


def local(
    inputs,
    lengths,
    gain_in,
    offset_in,
    conv_weight,
    gain_mid,
    offset_mid,
    point_weight,
    point_bias,
    cotangent,
):
    win_count, chan_local, count_of_bins = inputs.shape
    count_of_taps = conv_weight.shape[0]
    bottle = conv_weight.shape[2]
    bottle_local = bottle // lax.axis_size("ch")
    offset_at = lax.axis_index("ch") * bottle_local
    places = lax.axis_index("seq") * count_of_bins + jnp.arange(count_of_bins, dtype=jnp.int32)
    valid_rows = (places[None, :] < lengths[:, None]).astype(jnp.float32)[:, None, :]
    x_wide = inputs.astype(jnp.float32)
    sum_first = jnp.sum(valid_rows * x_wide, axis=(0, 2))
    sum_second = jnp.sum(valid_rows * x_wide * x_wide, axis=(0, 2))
    sum_first, sum_second, filled = lax.psum(
        (sum_first, sum_second, jnp.sum(valid_rows)), ("seq", "win")
    )
    mean_in = sum_first / filled
    scale_in = lax.rsqrt(sum_second / filled - mean_in * mean_in + EPS)
    norm_in = (x_wide - column(mean_in)) * column(scale_in)
    pre_in = norm_in * column(gain_in) + column(offset_in)
    input_activation, gelu_in_back = jax.vjp(jax.nn.gelu, pre_in)
    lowered_activation = (input_activation * valid_rows).astype(jnp.bfloat16)
    padded_input = with_halo(lowered_activation, (("seq", 2),), DILATION_BINS)
    stacked_taps = jnp.concatenate(
        [
            padded_input[
                :,
                :,
                kernel_tap_index * DILATION_BINS : kernel_tap_index * DILATION_BINS + count_of_bins,
            ]
            for kernel_tap_index in range(count_of_taps)
        ],
        axis=1,
    )
    flat_weight = conv_weight.reshape(count_of_taps * chan_local, bottle)
    partial_value = jnp.einsum(
        "wkt,kf->wft", stacked_taps, flat_weight, preferred_element_type=jnp.float32
    )
    conv_out = lax.psum_scatter(partial_value, "ch", scatter_dimension=1, tiled=True)
    gain_part = lax.dynamic_slice_in_dim(gain_mid, offset_at, bottle_local)
    offset_part = lax.dynamic_slice_in_dim(offset_mid, offset_at, bottle_local)
    mid_first, mid_second = norm_sums(
        jnp.sum(valid_rows * conv_out, axis=(0, 2)),
        jnp.sum(valid_rows * conv_out * conv_out, axis=(0, 2)),
    )
    mean_mid = mid_first / filled
    scale_mid = lax.rsqrt(mid_second / filled - mean_mid * mean_mid + EPS)
    norm_mid = (conv_out - column(mean_mid)) * column(scale_mid)
    pre_mid = norm_mid * column(gain_part) + column(offset_part)
    act_mid, gelu_mid_back = jax.vjp(jax.nn.gelu, pre_mid)
    act_mid_low = (act_mid * valid_rows).astype(jnp.bfloat16)
    mixed_in = lax.all_gather(act_mid_low, "ch", axis=1, tiled=True)
    branch = jnp.einsum("wft,fc->wct", mixed_in, point_weight, preferred_element_type=jnp.float32)
    outputs = (x_wide + branch + column(point_bias)).astype(jnp.bfloat16)
    grad_point = jnp.einsum("wft,wct->fc", mixed_in, cotangent, preferred_element_type=jnp.float32)
    grad_bias = jnp.sum(cotangent.astype(jnp.float32), axis=(0, 2))
    partial_back = jnp.einsum(
        "wct,fc->wft", cotangent, point_weight, preferred_element_type=jnp.float32
    )
    grad_act_mid = lax.psum_scatter(partial_back, "ch", scatter_dimension=1, tiled=True)
    grad_pre_mid = gelu_mid_back(grad_act_mid * valid_rows)[0]
    local_beta = jnp.sum(grad_pre_mid, axis=(0, 2))
    local_gamma = jnp.sum(grad_pre_mid * norm_mid, axis=(0, 2))
    grad_point, grad_bias, beta_mid, gamma_mid = lax.psum(
        (grad_point, grad_bias, local_beta, local_gamma), ("seq", "win")
    )
    grad_conv_out = column(gain_part * scale_mid) * (
        grad_pre_mid - valid_rows * (column(beta_mid) + norm_mid * column(gamma_mid)) / filled
    )
    grad_low = grad_conv_out.astype(jnp.bfloat16)
    complete_gradient = lax.all_gather(grad_low, "ch", axis=1, tiled=True)
    grad_conv = jnp.einsum(
        "wkt,wft->kf", stacked_taps, complete_gradient, preferred_element_type=jnp.float32
    )
    grad_conv = grad_conv.reshape(count_of_taps, chan_local, bottle)
    padded_gradient = with_halo(complete_gradient, (("seq", 2),), DILATION_BINS)
    back_taps = jnp.concatenate(
        [
            padded_gradient[
                :,
                :,
                (count_of_taps - 1 - kernel_tap_index)
                * DILATION_BINS : (count_of_taps - 1 - kernel_tap_index)
                * DILATION_BINS
                + count_of_bins,
            ]
            for kernel_tap_index in range(count_of_taps)
        ],
        axis=1,
    )
    back_weight = jnp.transpose(conv_weight, (0, 2, 1)).reshape(count_of_taps * bottle, chan_local)
    grad_act_in = jnp.einsum(
        "wkt,kc->wct", back_taps, back_weight, preferred_element_type=jnp.float32
    )
    grad_pre_in = gelu_in_back(grad_act_in * valid_rows)[0]
    local_beta_in = jnp.sum(grad_pre_in, axis=(0, 2))
    local_gamma_in = jnp.sum(grad_pre_in * norm_in, axis=(0, 2))
    grad_conv, beta_in, gamma_in = lax.psum(
        (grad_conv, local_beta_in, local_gamma_in), ("seq", "win")
    )
    grad_inputs = (
        cotangent.astype(jnp.float32)
        + column(gain_in * scale_in)
        * (grad_pre_in - valid_rows * (column(beta_in) + norm_in * column(gamma_in)) / filled)
    ).astype(jnp.bfloat16)
    return (
        outputs,
        grad_inputs,
        gamma_in,
        beta_in,
        grad_conv,
        gamma_mid,
        beta_mid,
        grad_point,
        grad_bias,
    )


def solution(mesh):
    return jax.shard_map(
        local,
        mesh=mesh,
        in_specs=(
            P("win", "ch", "seq"),
            P("win"),
            P("ch"),
            P("ch"),
            P(None, "ch", None),
            P(),
            P(),
            P(None, "ch"),
            P("ch"),
            P("win", "ch", "seq"),
        ),
        out_specs=(
            P("win", "ch", "seq"),
            P("win", "ch", "seq"),
            P("ch"),
            P("ch"),
            P(None, "ch", None),
            P("ch"),
            P("ch"),
            P(None, "ch"),
            P("ch"),
        ),
        check_vma=False,
    )
```

profile of v0, /device:TPU:0, one launch (start us, length us, event | category | flops | bytes accessed | tf_op | source)
XLA Modules:
  0.0 1546.0 jit_solution(16016527854371169664)
XLA Ops:
  9.4 12.6 copy.70
  28.7 36.1 %all-reduce.5 = (f32[384]{0:T(512)S(1)}, f32[]{:T(128)}, f32[384]{0:T(512)S(1)}) all-reduce(f32[384]{0:T(512)S(1)} %get-tuple-element.59, f32[]{:T(128)} %convert_reduce_fusion.1, f32[384]{0:T(512)S(1)} %get-tuple-element.58), channel_id=1, replica_groups=mesh['seq'=8,'ch'=2,'win'=2] {'seq','win'}, use_global_device_ids=true, to_apply=%region_5.0 | all-reduce | flops 769 | bytes 6152 | tf_op jit(solution)/shard_map/psum | solution.py:59
  66.1 11.2 fusion.28
  90.1 28.4 %copy.78 = f32[4,384,3072]{2,0,1:T(4,128)} copy(f32[4,384,3072]{2,1,0:T(8,128)S(1)} %convolution_bitcast_fusion) | data formatting | bytes 37748736 | tf_op jit(solution)/shard_map/wct,fc->wft/transpose | solution.py:102
  118.5 34.5 %convolution_bitcast_fusion.1 = f32[4,384,3072]{1,2,0:T(8,128)} fusion(bf16[1152,384,1]{1,0,2:T(8,128)(2,1)S(1)} %bitcast.41, bf16[4,384,57]{1,2,0:T(8,128)(2,1)S(1)} %collective-permute-done.1, bf16[4,384,3072]{1,2,0:T(8,128)(2,1)} %copy-done.2, bf16[4,384,57]{1,2,0:T(8,128)(2,1)S(1)} %collective-permute-done), kind=kOutput, calls=%fused_computation.72 | convolution fusion | flops 11013193728 | bytes 29546496 | tf_op jit(solution)/shard_map/wkt,kf->wft/dot_general | solution.py:81
  153.0 22.7 %copy.71 = f32[4,384,3072]{2,0,1:T(4,128)} copy(f32[4,384,3072]{1,2,0:T(8,128)} %convolution_bitcast_fusion.1) | data formatting | bytes 37748736 | tf_op jit(solution)/shard_map/wkt,kf->wft/transpose | solution.py:81
  177.7 825.7 %all-reduce.13.cloned.1.call-done = (f32[4,384,3072]{2,0,1:T(4,128)}, f32[4,384,3072]{2,0,1:T(4,128)}) async-done(((f32[4,384,3072]{2,0,1:T(4,128)}, f32[4,384,3072]{2,0,1:T(4,128)}), (f32[4,384,3072]{2,0,1:T(4,128)}, f32[4,384,3072]{2,0,1:T(4,128)})) %all-reduce.13.cloned.1.call-update) | async-done | bytes 37748752
  1003.5 11.6 constant_dynamic-slice_fusion
  1025.0 33.2 %all-reduce.4 = (f32[192]{0:T(256)S(1)}, f32[192]{0:T(256)S(1)}) all-reduce(f32[192]{0:T(256)S(1)} %get-tuple-element.57, f32[192]{0:T(256)S(1)} %get-tuple-element.56), channel_id=1, replica_groups=mesh['seq'=8,'ch'=2,'win'=2] {'seq','win'}, use_global_device_ids=true, to_apply=%region_8.0 | all-reduce | flops 384 | bytes 3072 | tf_op jit(solution)/shard_map/psum | solution.py:30
  1059.0 16.0 %fusion.66 = (f32[192]{0:T(256)S(1)}, f32[192]{0:T(256)S(1)}, f32[4,192,3072]{2,1,0:T(8,128)}, bf16[4,192,3072]{2,1,0:T(8,128)(2,1)}) fusion(f32[192]{0:T(256)S(1)} %get-tuple-element.79, f32[192]{0:T(256)S(1)} %get-tuple-element.80, f32[4,192,3072]{2,0,1:T(4,128)} %copy-done.1, f32[192]{0:T(256)S(1)} %dynamic_slice.7, f32[192]{0:T(256)S(1)} %get-tuple-element.81, ...), kind=kLoop, calls=%fused_computation.92 | loop fusion | flops 70778496 | bytes 33083904 | tf_op jit(solution)/shard_map/reduce_sum | solution.py:107
  1075.0 29.9 %all-reduce.3 = (f32[192]{0:T(256)S(1)}, f32[192]{0:T(256)S(1)}) all-reduce(f32[192]{0:T(256)S(1)} %get-tuple-element.61, f32[192]{0:T(256)S(1)} %get-tuple-element.60), channel_id=1, replica_groups=mesh['seq'=8,'ch'=2,'win'=2] {'seq','win'}, use_global_device_ids=true, to_apply=%region_15.0 | all-reduce | flops 384 | bytes 3072 | tf_op jit(solution)/shard_map/psum | solution.py:109
  1104.9 11.5 multiply_convert_fusion
  1133.4 13.0 copy.77
  1152.4 88.1 %all-gather.5.cloned.1.call-done = bf16[4,384,3072]{2,0,1:T(4,128)(2,1)} async-done(((bf16[4,192,3072]{2,0,1:T(4,128)(2,1)}), bf16[4,384,3072]{2,0,1:T(4,128)(2,1)}) %all-gather.5.cloned.1.call-update) | async-done | bytes 9437200 | tf_op jit(solution)/shard_map/all_gather | solution.py:116
  1240.5 16.9 %copy.82 = bf16[4,384,3072]{1,2,0:T(8,128)(2,1)} copy(bf16[4,384,3072]{2,0,1:T(4,128)(2,1)} %all-gather.5.cloned.1.call-done) | data formatting | bytes 18874368 | tf_op jit(solution)/shard_map/all_gather | solution.py:116
  1262.9 56.3 %fusion.52 = f32[1152,384,1]{1,0,2:T(8,128)} fusion(bf16[4,384,3072]{1,2,0:T(8,128)(2,1)} %copy.82, bf16[4,384,57]{1,2,0:T(8,128)(2,1)S(1)} %collective-permute-done.1, bf16[4,384,3072]{1,2,0:T(8,128)(2,1)} %copy-done.2, bf16[4,384,57]{1,2,0:T(8,128)(2,1)S(1)} %collective-permute-done), kind=kOutput, calls=%fused_computation.73 | convolution fusion | flops 11013193728 | bytes 20994048 | tf_op jit(solution)/shard_map/wkt,wft->kf/dot_general | solution.py:117
  1319.2 41.0 %all-gather.3.cloned.1.call-done = bf16[4,384,3072]{2,0,1:T(4,128)(2,1)} async-done(((bf16[4,192,3072]{2,0,1:T(4,128)(2,1)}), bf16[4,384,3072]{2,0,1:T(4,128)(2,1)}) %all-gather.3.cloned.1.call-update) | async-done | bytes 9437200 | tf_op jit(solution)/shard_map/all_gather | solution.py:97
  1360.2 28.9 %fusion.37 = bf16[4,384,3072]{1,2,0:T(8,128)(2,1)} fusion(bf16[4,384,3072]{1,2,0:T(8,128)(2,1)} %copy.70, f32[384]{0:T(512)S(1)} %copy-done.21, bf16[4,384,3072]{2,0,1:T(4,128)(2,1)} %all-gather.3.cloned.1.call-done, bf16[384,384]{1,0:T(8,128)(2,1)S(1)} %copy-done), kind=kOutput, calls=%fused_computation.47 | convolution fusion | flops 3642753024 | bytes 28608000 | tf_op jit(solution)/shard_map/wft,fc->wct/dot_general | solution.py:98
  1389.1 9.3 fusion.57
  1398.4 12.6 copy.90
  1411.1 57.0 %fusion.65 = (f32[384]{0:T(512)S(1)}, f32[384]{0:T(512)S(1)}, f32[4,384,3072]{1,2,0:T(8,128)}) fusion(f32[384]{0:T(512)S(1)} %copy-done.5, f32[384]{0:T(512)S(1)} %copy-done.7, bf16[4,384,3072]{1,2,0:T(8,128)(2,1)} %copy.70, f32[384]{0:T(512)S(1)} %copy-done.13, f32[384]{0:T(512)S(1)} %copy-done.9, f32[4,3072]{1,0:T(4,128)S(1)} %compare_convert_fusion, ...), kind=kOutput, calls=%fused_computation.91 | convolution fusion | flops 11145314304 | bytes 39042048 | tf_op jit(solution)/shard_map/wkt,kc->wct/dot_general | solution.py:137
  1468.1 34.8 %all-reduce.2 = (f32[384]{0:T(512)S(1)}, f32[384]{0:T(512)S(1)}, f32[384]{0:T(512)}) all-reduce(f32[384]{0:T(512)S(1)} %get-tuple-element.55, f32[384]{0:T(512)S(1)} %get-tuple-element.54, f32[384]{0:T(512)S(1)} %copy-done.11), channel_id=1, replica_groups=mesh['seq'=8,'ch'=2,'win'=2] {'seq','win'}, use_global_device_ids=true, to_apply=%region_19.0 | all-reduce | flops 1152 | bytes 9216 | tf_op jit(solution)/shard_map/psum | solution.py:143
  1502.9 19.0 %fusion.11 = bf16[4,384,3072]{1,2,0:T(8,128)(2,1)} fusion(bf16[4,384,3072]{1,2,0:T(8,128)(2,1)} %copy.77, f32[4,384,3072]{1,2,0:T(8,128)} %get-tuple-element.89, bf16[4,384,3072]{1,2,0:T(8,128)(2,1)} %copy.70, f32[]{:T(128)} %get-tuple-element.70, f32[384]{0:T(512)S(1)} %get-tuple-element.94, f32[384]{0:T(512)S(1)} %get-tuple-element.95, ...), kind=kLoop, calls=%fused_computation.21 | loop fusion | flops 56623104 | bytes 47242756 | tf_op jit(solution)/shard_map/convert_element_type | solution.py:150
  1521.9 12.6 copy.91
  (81 shorter events, 68.1 us)
Async XLA Ops:
  7.2 75.4 %copy-start = (bf16[384,384]{1,0:T(8,128)(2,1)S(1)}, bf16[384,384]{1,0:T(8,128)(2,1)}, u32[]{:S(2)}) copy-start(bf16[384,384]{1,0:T(8,128)(2,1)} %param.17) | copy-start | bytes 884740
  7.2 57.6 %copy-start.8 = (f32[384]{0:T(512)S(1)}, f32[384]{0:T(512)}, u32[]{:S(2)}) copy-start(f32[384]{0:T(512)} %param.12) | copy-start | bytes 4612
  7.2 58.9 %copy-start.12 = (f32[384]{0:T(512)S(1)}, f32[384]{0:T(512)}, u32[]{:S(2)}) copy-start(f32[384]{0:T(512)} %param.13) | copy-start | bytes 4612
  7.2 996.2 %all-reduce.13.cloned.1.call-start = ((), (), s32[]{:S(2)}) async-start(), calls=%async_computation.3 | async-start | bytes 75497472
  77.4 41.1 %collective-permute-start = (bf16[4,384,57]{1,2,0:T(8,128)(2,1)S(1)}, bf16[4,384,57]{1,2,0:T(8,128)(2,1)S(1)}, u32[]{:S(2)}, u32[]{:S(2)}) collective-permute-start(bf16[4,384,57]{1,2,0:T(8,128)(2,1)S(1)} %get-tuple-element.86), channel_id=1, source_target_pairs={{0,4},{4,8},{8,12},{12,16},{16,20},{20,24},{24,28},{1,5},{5,9},{9,... | collective-permute-start | bytes 525320 | tf_op jit(solution)/shard_map/ppermute | solution.py:20
  81.1 37.4 %collective-permute-start.1 = (bf16[4,384,57]{1,2,0:T(8,128)(2,1)S(1)}, bf16[4,384,57]{1,2,0:T(8,128)(2,1)S(1)}, u32[]{:S(2)}, u32[]{:S(2)}) collective-permute-start(bf16[4,384,57]{1,2,0:T(8,128)(2,1)S(1)} %get-tuple-element.87), channel_id=1, source_target_pairs={{4,0},{8,4},{12,8},{16,12},{20,16},{24,20},{28,24},{5,1},{9,5},{13... | collective-permute-start | bytes 525320 | tf_op jit(solution)/shard_map/ppermute | solution.py:22
  90.1 28.4 %copy-start.3 = (bf16[3,384,384]{2,1,0:T(8,128)(2,1)S(1)}, bf16[3,384,384]{2,1,0:T(8,128)(2,1)}, u32[]{:S(2)}) copy-start(bf16[3,384,384]{2,1,0:T(8,128)(2,1)} %param.14) | copy-start | bytes 2654212
  175.8 1064.7 %all-gather.5.cloned.1.call-start = ((), (), s32[]{:S(2)}) async-start(), calls=%async_computation.1 | async-start | bytes 14155776 | tf_op jit(solution)/shard_map/all_gather | solution.py:116
  1003.5 54.8 %copy-start.19 = (f32[384]{0:T(512)S(1)}, f32[384]{0:T(512)}, u32[]{:S(2)}) copy-start(f32[384]{0:T(512)} %param.15) | copy-start | bytes 4612
  1104.9 17.4 %copy-start.17 = (f32[192]{0:T(256)}, f32[192]{0:T(256)S(1)}, u32[]{:S(2)}) copy-start(f32[192]{0:T(256)S(1)} %get-tuple-element.98) | copy-start | bytes 2308
  1122.3 237.9 %all-gather.3.cloned.1.call-start = ((), (), s32[]{:S(2)}) async-start(), calls=%async_computation | async-start | bytes 14155776 | tf_op jit(solution)/shard_map/all_gather | solution.py:97
  1130.9 403.7 %all-reduce.11.cloned.1.call-start = ((), (), s32[]{:S(2)}) async-start(), calls=%async_computation.2 | async-start | bytes 4718592 | tf_op jit(solution)/shard_map/psum | solution.py:143
  1258.5 152.5 %collective-permute-start.2 = (bf16[4,384,57]{1,2,0:T(8,128)(2,1)S(1)}, bf16[4,384,57]{1,2,0:T(8,128)(2,1)S(1)}, u32[]{:S(2)}, u32[]{:S(2)}) collective-permute-start(bf16[4,384,57]{1,2,0:T(8,128)(2,1)S(1)} %get-tuple-element.84), channel_id=1, source_target_pairs={{4,0},{8,4},{12,8},{16,12},{20,16},{24,20},{28,24},{5,1},{9,5},{13... | collective-permute-start | bytes 525320 | tf_op jit(solution)/shard_map/ppermute | solution.py:22
  1259.8 100.4 %copy-start.21 = (f32[384]{0:T(512)S(1)}, f32[384]{0:T(512)}, u32[]{:S(2)}) copy-start(f32[384]{0:T(512)} %param.18) | copy-start | bytes 4612
  1259.8 151.2 %collective-permute-start.3 = (bf16[4,384,57]{1,2,0:T(8,128)(2,1)S(1)}, bf16[4,384,57]{1,2,0:T(8,128)(2,1)S(1)}, u32[]{:S(2)}, u32[]{:S(2)}) collective-permute-start(bf16[4,384,57]{1,2,0:T(8,128)(2,1)S(1)} %get-tuple-element.85), channel_id=1, source_target_pairs={{0,4},{4,8},{8,12},{12,16},{16,20},{20,24},{24,28},{1,5},{5,9},{9,... | collective-permute-start | bytes 525320 | tf_op jit(solution)/shard_map/ppermute | solution.py:20
  1360.2 28.9 %copy-start.20 = (bf16[4,384,3072]{2,0,1:T(4,128)(2,1)S(1)}, bf16[4,384,3072]{2,0,1:T(4,128)(2,1)}, u32[]{:S(2)}) copy-start(bf16[4,384,3072]{2,0,1:T(4,128)(2,1)} %all-gather.3.cloned.1.call-done) | copy-start | bytes 28311556
  1389.1 21.9 %copy-start.5 = (f32[384]{0:T(512)S(1)}, f32[384]{0:T(512)}, u32[]{:S(2)}) copy-start(f32[384]{0:T(512)} %copy-done.4) | copy-start | bytes 4612
  1389.1 21.9 %copy-start.7 = (f32[384]{0:T(512)S(1)}, f32[384]{0:T(512)}, u32[]{:S(2)}) copy-start(f32[384]{0:T(512)} %copy-done.6) | copy-start | bytes 4612
  1389.1 21.9 %copy-start.9 = (f32[384]{0:T(512)S(1)}, f32[384]{0:T(512)}, u32[]{:S(2)}) copy-start(f32[384]{0:T(512)} %param.12) | copy-start | bytes 4612
  1389.1 21.9 %copy-start.13 = (f32[384]{0:T(512)S(1)}, f32[384]{0:T(512)}, u32[]{:S(2)}) copy-start(f32[384]{0:T(512)} %param.13) | copy-start | bytes 4612
  1411.1 57.0 %copy-start.11 = (f32[384]{0:T(512)S(1)}, f32[384]{0:T(512)}, u32[]{:S(2)}) copy-start(f32[384]{0:T(512)} %convert_reduce_fusion) | copy-start | bytes 4612
  1411.1 91.8 %copy-start.10 = (f32[384]{0:T(512)S(1)}, f32[384]{0:T(512)}, u32[]{:S(2)}) copy-start(f32[384]{0:T(512)} %get-tuple-element.76) | copy-start | bytes 4612
  1502.9 19.0 %copy-start.14 = (f32[384]{0:T(512)}, f32[384]{0:T(512)S(1)}, u32[]{:S(2)}) copy-start(f32[384]{0:T(512)S(1)} %get-tuple-element.94) | copy-start | bytes 4612
  1502.9 19.0 %copy-start.15 = (f32[384]{0:T(512)}, f32[384]{0:T(512)S(1)}, u32[]{:S(2)}) copy-start(f32[384]{0:T(512)S(1)} %get-tuple-element.95) | copy-start | bytes 4612
  (7 other events, 52.5 us)
Sparse Core Ops, SparseCore 0:
  175.9 827.5 all-reduce.12
  1122.4 118.0 all-gather.4
  1242.1 118.0 all-gather.2
  1411.1 99.6 all-reduce.10
where the time goes:
time: 1550 us
  waiting for transfers between devices  955 us (62%)
  matrix products  194 us (13%)
  local copies, waits for them, and re-layouts  160 us (10%)
  blocking collectives  134 us (9%)
  other arithmetic  80.8 us (5%)
    unnamed x5, waiting for transfers between devices  826 us
    all_gather x1, waiting for transfers between devices, local(): complete_gradient = lax.all_gather(grad_low, 'ch', axis=1, tiled=True)  88.1 us
    unnamed x55, local copies, waits for them, and re-layouts  76.6 us
    dot_general x1, matrix products, local(): jnp.einsum('wkt,kc->wct', back_taps, back_weight, preferred_element_type=...  57 us
    dot_general x1, matrix products, local(): jnp.einsum('wkt,wft->kf', stacked_taps, complete_gradient, preferred_elem...  56.3 us
    all_gather x1, waiting for transfers between devices, local(): mixed_in = lax.all_gather(act_mid_low, 'ch', axis=1, tiled=True)  41 us
    psum x1, blocking collectives, local(): lax.psum((sum_first, sum_second, jnp.sum(valid_rows)), ('seq', 'win'))  36.1 us
    psum x1, blocking collectives, local(): lax.psum((grad_conv, local_beta_in, local_gamma_in), ('seq', 'win'))  34.8 us
  transfers between devices with their start and end apart: 8, of which 3 were waited for; matrix products, arithmetic and copies ran while one was open for 18% of the time, Pallas kernels for 0%

commit v1 on v0

--- a/solution.py
+++ b/solution.py
@@ -1,12 +1,19 @@
+import functools
+
 import jax
 import jax.numpy as jnp
 from jax import lax
+from jax.experimental import pallas as pl
+from jax.experimental.pallas import tpu as pltpu
 from jax.sharding import PartitionSpec as P
 
 DILATION_BINS = 57
 
 
 EPS = 1e-05
+LANES = 128
+TILE = 384
+VMEM_BYTES = 48 * 1024 * 1024
 
 
 def with_halo(cells, sides, width):
@@ -34,7 +41,7 @@
     return vector[:, None]
 
 
-def local(
+def local_any(
     inputs,
     lengths,
     gain_in,
@@ -161,7 +168,586 @@
     )
 
 
+def params(flops, moved):
+    return dict(
+        compiler_params=pltpu.CompilerParams(vmem_limit_bytes=VMEM_BYTES),
+        cost_estimate=pl.CostEstimate(flops=flops, bytes_accessed=moved, transcendentals=0),
+    )
+
+
+def dot(a, b):
+    return jnp.dot(a, b, preferred_element_type=jnp.float32)
+
+
+def dot_t(a, b):
+    return lax.dot_general(a, b, (((1,), (1,)), ((), ())), preferred_element_type=jnp.float32)
+
+
+def lane_sum(cells):
+    total = cells[:, :LANES]
+    for at in range(LANES, cells.shape[1], LANES):
+        total = total + cells[:, at : at + LANES]
+    return total
+
+
+GELU_A = 0.7978845608028654
+GELU_B = 0.044715
+
+
+def gelu(v):
+    return 0.5 * v * (1.0 + jnp.tanh(GELU_A * (v + GELU_B * (v * v * v))))
+
+
+def gelu_slope(v):
+    square = v * v
+    th = jnp.tanh(GELU_A * (v + GELU_B * (v * square)))
+    return 0.5 * (1.0 + th) + 0.5 * v * (1.0 - th * th) * (GELU_A * (1.0 + 3.0 * GELU_B * square))
+
+
+def ext_start(tile, tiles):
+    first, second, _ = tiles
+    extra = jnp.where(tile >= first, 2 * LANES, 0) + jnp.where(tile >= first + second, 2 * LANES, 0)
+    return pl.multiple_of(tile * TILE + extra, LANES)
+
+
+def fill_taps(cat, refs, start):
+    chans = refs[0].shape[0]
+    row = 0
+    for ref in refs:
+        wide = ref[:, pl.ds(start, TILE + 2 * LANES)]
+        for tap in range(3):
+            at = LANES + (tap - 1) * DILATION_BINS
+            cat[row : row + chans, :] = wide[:, at : at + TILE]
+            row += chans
+
+
+def conv_kernel(tiles, own, other, weight, valid, out, first, second, cat):
+    tile = pl.program_id(0)
+    fill_taps(cat, (own, other), ext_start(tile, tiles))
+    acc = dot(weight[...], cat[...])
+    out[...] = acc
+    kept = acc * valid[...]
+
+    @pl.when(tile == 0)
+    def _():
+        first[...] = jnp.zeros_like(first)
+        second[...] = jnp.zeros_like(second)
+
+    first[...] += lane_sum(kept)
+    second[...] += lane_sum(kept * acc)
+
+
+def conv_forward(own, other, weight, valid, tiles):
+    chans, wide = own.shape
+    bottle, depth = weight.shape
+    count = sum(tiles)
+    whole = lambda shape: pl.BlockSpec(shape, lambda i: (0, 0))
+    return pl.pallas_call(
+        functools.partial(conv_kernel, tiles),
+        grid=(count,),
+        in_specs=[
+            whole((chans, wide)),
+            whole((chans, wide)),
+            whole((bottle, depth)),
+            pl.BlockSpec((1, TILE), lambda i: (0, i)),
+        ],
+        out_specs=[
+            pl.BlockSpec((bottle, TILE), lambda i: (0, i)),
+            whole((bottle, LANES)),
+            whole((bottle, LANES)),
+        ],
+        out_shape=[
+            jax.ShapeDtypeStruct((bottle, count * TILE), jnp.float32),
+            jax.ShapeDtypeStruct((bottle, LANES), jnp.float32),
+            jax.ShapeDtypeStruct((bottle, LANES), jnp.float32),
+        ],
+        scratch_shapes=[pltpu.VMEM((depth, TILE), jnp.bfloat16)],
+        **params(2 * bottle * depth * count * TILE, 4 * bottle * count * TILE + 4 * chans * wide),
+    )(own, other, weight, valid)
+
+
+def mid_kernel(conv, act, valid, own, other, point, cols, grad, beta, gamma, outer):
+    chans = own.shape[0]
+    mean, scale, gain, offset = (cols[:, i : i + 1] for i in range(4))
+    back = dot(point[:, :chans], own[...]) + dot(point[:, chans:], other[...])
+    norm = (conv[...] - mean) * scale
+    part = valid[...] * gelu_slope(norm * gain + offset) * back
+    grad[...] = part
+
+    @pl.when(pl.program_id(0) == 0)
+    def _():
+        beta[...] = jnp.zeros_like(beta)
+        gamma[...] = jnp.zeros_like(gamma)
+        outer[...] = jnp.zeros_like(outer)
+
+    beta[...] += lane_sum(part)
+    gamma[...] += lane_sum(part * norm)
+    outer[:, :chans] += dot_t(act[...], own[...])
+    outer[:, chans:] += dot_t(act[...], other[...])
+
+
+def mid_back(conv, act, valid, own, other, point, cols, base):
+    bottle = conv.shape[0]
+    chans, bins = own.shape
+    count = bins // TILE
+    whole = lambda shape: pl.BlockSpec(shape, lambda i: (0, 0))
+    shifted = lambda rows: pl.BlockSpec((rows, TILE), lambda i: (0, i + base))
+    plain = lambda rows: pl.BlockSpec((rows, TILE), lambda i: (0, i))
+    return pl.pallas_call(
+        mid_kernel,
+        grid=(count,),
+        in_specs=[
+            shifted(bottle),
+            shifted(bottle),
+            shifted(1),
+            plain(chans),
+            plain(chans),
+            whole(point.shape),
+            whole(cols.shape),
+        ],
+        out_specs=[
+            plain(bottle),
+            whole((bottle, LANES)),
+            whole((bottle, LANES)),
+            whole((bottle, 2 * chans)),
+        ],
+        out_shape=[
+            jax.ShapeDtypeStruct((bottle, bins), jnp.float32),
+            jax.ShapeDtypeStruct((bottle, LANES), jnp.float32),
+            jax.ShapeDtypeStruct((bottle, LANES), jnp.float32),
+            jax.ShapeDtypeStruct((bottle, 2 * chans), jnp.float32),
+        ],
+        **params(8 * bottle * chans * bins, (10 * bottle + 4 * chans) * bins),
+    )(conv, act, valid, own, other, point, cols)
+
+
+def weight_kernel(tiles, own, other, near, far, out, cat):
+    tile = pl.program_id(0)
+    fill_taps(cat, (own, other), ext_start(tile, tiles))
+
+    @pl.when(tile == 0)
+    def _():
+        out[...] = jnp.zeros_like(out)
+
+    @pl.when(tile < tiles[0])
+    def _():
+        out[...] += dot_t(cat[...], near[...])
+
+    @pl.when(tile >= tiles[0])
+    def _():
+        out[...] += dot_t(cat[...], far[...])
+
+
+def conv_weight_back(own, other, near, far, tiles):
+    chans, wide = own.shape
+    bottle = near.shape[0]
+    depth = 6 * chans
+    count = sum(tiles)
+    whole = lambda shape: pl.BlockSpec(shape, lambda i: (0, 0))
+    return pl.pallas_call(
+        functools.partial(weight_kernel, tiles),
+        grid=(count,),
+        in_specs=[
+            whole((chans, wide)),
+            whole((chans, wide)),
+            pl.BlockSpec((bottle, TILE), lambda i: (0, jnp.minimum(i, tiles[0] - 1))),
+            pl.BlockSpec((bottle, TILE), lambda i: (0, jnp.maximum(i - tiles[0], 0))),
+        ],
+        out_specs=whole((depth, bottle)),
+        out_shape=jax.ShapeDtypeStruct((depth, bottle), jnp.float32),
+        scratch_shapes=[pltpu.VMEM((depth, TILE), jnp.bfloat16)],
+        **params(2 * bottle * depth * count * TILE, 4 * chans * wide),
+    )(own, other, near, far)
+
+
+def out_kernel(place, act, x, weight, bias, *rest):
+    out = rest[-1]
+    out[0] = (x[0].astype(jnp.float32) + dot(weight[...], act[...]) + bias[...]).astype(out.dtype)
+
+
+def write_outputs(prev, act, count, place, x, weight, bias):
+    windows, chans, bins = x.shape
+    bottle = act.shape[0]
+    tile = 2 * TILE
+    at = pl.BlockSpec((1, chans, tile), lambda i, p: (p[0], 0, p[1] + i))
+    whole = lambda shape: pl.BlockSpec(shape, lambda i, p: (0, 0))
+    in_specs = [
+        pl.BlockSpec((bottle, tile), lambda i, p: (0, i)),
+        at,
+        whole((chans, bottle)),
+        whole((chans, 1)),
+    ]
+    operands = [place, act, x, weight, bias]
+    aliases = {}
+    if prev is not None:
+        in_specs.append(pl.BlockSpec(memory_space=pl.ANY))
+        operands.append(prev)
+        aliases = {5: 0}
+    return pl.pallas_call(
+        out_kernel,
+        grid_spec=pltpu.PrefetchScalarGridSpec(
+            num_scalar_prefetch=1, grid=(count,), in_specs=in_specs, out_specs=at
+        ),
+        out_shape=jax.ShapeDtypeStruct(x.shape, x.dtype),
+        input_output_aliases=aliases,
+        **params(2 * bottle * chans * count * tile, (4 * chans + 2 * bottle) * count * tile),
+    )(*operands)
+
+
+def back_kernel(order, grads, x, valid, weight, cols, out, beta, gamma, cat):
+    bottle = grads.shape[1]
+    start = pl.multiple_of(pl.program_id(1) * TILE, LANES)
+    wide = grads[0, :, pl.ds(start, TILE + 2 * LANES)]
+    for tap in range(3):
+        at = LANES - (tap - 1) * DILATION_BINS
+        cat[tap * bottle : (tap + 1) * bottle, :] = wide[:, at : at + TILE]
+    mean, scale, gain, offset = (cols[:, i : i + 1] for i in range(4))
+    norm = (x[0].astype(jnp.float32) - mean) * scale
+    part = valid[0] * gelu_slope(norm * gain + offset) * dot(weight[...], cat[...])
+    out[0] = part
+
+    @pl.when((pl.program_id(0) == 0) & (pl.program_id(1) == 0))
+    def _():
+        beta[...] = jnp.zeros_like(beta)
+        gamma[...] = jnp.zeros_like(gamma)
+
+    beta[...] += lane_sum(part)
+    gamma[...] += lane_sum(part * norm)
+
+
+def input_back(order, grads, x, valid, weight, cols):
+    windows, chans, bins = x.shape
+    bottle, wide = grads.shape[1:]
+    at = pl.BlockSpec((1, chans, TILE), lambda w, i, p: (p[w], 0, i))
+    whole = lambda shape: pl.BlockSpec(shape, lambda w, i, p: (0, 0))
+    return pl.pallas_call(
+        back_kernel,
+        grid_spec=pltpu.PrefetchScalarGridSpec(
+            num_scalar_prefetch=1,
+            grid=(windows, bins // TILE),
+            in_specs=[
+                pl.BlockSpec((1, bottle, wide), lambda w, i, p: (w, 0, 0)),
+                at,
+                pl.BlockSpec((1, 1, TILE), lambda w, i, p: (w, 0, i)),
+                whole(weight.shape),
+                whole(cols.shape),
+            ],
+            out_specs=[at, whole((chans, LANES)), whole((chans, LANES))],
+            scratch_shapes=[pltpu.VMEM((3 * bottle, TILE), jnp.bfloat16)],
+        ),
+        out_shape=[
+            jax.ShapeDtypeStruct(x.shape, jnp.float32),
+            jax.ShapeDtypeStruct((chans, LANES), jnp.float32),
+            jax.ShapeDtypeStruct((chans, LANES), jnp.float32),
+        ],
+        **params(6 * bottle * chans * windows * bins, 6 * chans * windows * bins),
+    )(order, grads, x, valid, weight, cols)
+
+
+def after(cells, done):
+    spot = lax.slice(done, (0,) * done.ndim, (1,) * done.ndim).reshape(())
+    return cells + (spot * 0).astype(cells.dtype)
+
+
+def local_pair(
+    inputs,
+    lengths,
+    gain_in,
+    offset_in,
+    conv_weight,
+    gain_mid,
+    offset_mid,
+    point_weight,
+    point_bias,
+    cotangent,
+):
+    windows, chans, bins = inputs.shape
+    taps, _, bottle = conv_weight.shape
+    count_seq, count_win = lax.axis_size("seq"), lax.axis_size("win")
+    side, shard, group_at = (lax.axis_index(name) for name in ("ch", "seq", "win"))
+    quarter = count_seq // 4
+    group = shard // quarter
+    piece, half, eighth = bins // 4, bins // 2, bins // 8
+    tiles = (bins // TILE, half // TILE, eighth // TILE)
+    axes = ("seq", "ch", "win")
+    swap = [(0, 1), (1, 0)]
+    over = lambda cells: lax.ppermute(cells, "ch", swap)
+    low_lanes = lax.broadcasted_iota(jnp.int32, (1, LANES), 1) < LANES // 2
+
+    ids = jnp.arange(windows, dtype=jnp.int32)
+    ahead = (lengths[None, :] > lengths[:, None]) | (
+        (lengths[None, :] == lengths[:, None]) & (ids[None, :] < ids[:, None])
+    )
+    rank = jnp.sum(ahead.astype(jnp.int32), axis=1)
+    chosen = rank[None, :] == ids[:, None]
+    order = jnp.sum(jnp.where(chosen, ids[None, :], 0), axis=1)
+    ranked = jnp.sum(jnp.where(chosen, lengths[None, :], 0), axis=1)
+    pick = lambda cells, slot: lax.dynamic_index_in_dim(cells, order[slot], 0, keepdims=False)
+    by_side = lambda role, first, second: jnp.where(role == 0, first, second)
+
+    x1_mine = pick(inputs, side)
+    x1_other = over(pick(inputs, 1 - side))
+
+    flat = jnp.concatenate([conv_weight.reshape(taps * chans, bottle), point_weight], axis=0)
+    share = flat.shape[0] // (count_seq * count_win)
+    device_at = group_at * count_seq + shard
+    flat_other = lax.all_gather(
+        over(lax.dynamic_slice_in_dim(flat, device_at * share, share, 0)),
+        ("win", "seq"),
+        axis=0,
+        tiled=True,
+    )
+    conv_other = flat_other[: taps * chans].reshape(taps, chans, bottle)
+    point_other = flat_other[taps * chans :]
+
+    ends = [(i, i + 1) for i in range(count_seq - 1)]
+    back_ends = [(i + 1, i) for i in range(count_seq - 1)]
+
+    def halo_of(cells):
+        right = lax.ppermute(cells[..., :LANES], "seq", back_ends)
+        left = lax.ppermute(cells[..., -LANES:], "seq", ends)
+        return jnp.where(low_lanes, right, left)
+
+    halo = halo_of(inputs)
+
+    def spread(parts):
+        total = jnp.where(group == 0, parts[0], jnp.zeros_like(parts[0]))
+        for k in range(1, 4):
+            total = total + lax.ppermute(parts[k], "seq", [(i, i + k * quarter) for i in range(quarter)])
+        return total
+
+    def collect(cells):
+        parts = [jnp.where(group == 0, cells, jnp.zeros_like(cells))]
+        for k in range(1, 4):
+            parts.append(lax.ppermute(cells, "seq", [(i + k * quarter, i) for i in range(quarter)]))
+        return jnp.concatenate(parts, axis=1)
+
+    quarter_x, quarter_halo = pick(inputs, 3), pick(halo, 3)
+    wide_x = jnp.concatenate([quarter_halo, quarter_x, quarter_halo], axis=1)
+
+    def piece_of(k):
+        right = wide_x[:, LANES + piece * (k + 1) : 2 * LANES + piece * (k + 1)]
+        left = wide_x[:, piece * k : LANES + piece * k]
+        return jnp.concatenate(
+            [jnp.where(low_lanes, right, left), quarter_x[:, piece * k : piece * (k + 1)]], axis=1
+        )
+
+    extra_x = spread([piece_of(k) for k in range(4)])
+    third_x, third_halo = pick(inputs, 2), pick(halo, 2)
+
+    def second_part(role):
+        e, e_halo = extra_x[:, LANES:], extra_x[:, :LANES]
+        h2 = by_side(
+            role,
+            jnp.where(low_lanes, third_x[:, half : half + LANES], third_halo),
+            jnp.where(low_lanes, third_halo, third_x[:, half - LANES : half]),
+        )
+        h3 = by_side(
+            role,
+            jnp.where(low_lanes, e[:, eighth : eighth + LANES], e_halo),
+            jnp.where(low_lanes, e_halo, e[:, eighth - LANES : eighth]),
+        )
+        s2 = by_side(role, third_x[:, :half], third_x[:, half:])
+        s3 = by_side(role, e[:, :eighth], e[:, eighth:])
+        return jnp.concatenate([pick(halo, role), h2, h3, s2, s3], axis=1)
+
+    x2_mine = second_part(side)
+    x2_other = over(second_part(1 - side))
+
+    extra_c = spread([pick(cotangent, 3)[:, piece * k : piece * (k + 1)] for k in range(4)])
+    third_c = pick(cotangent, 2)
+
+    def second_cot(role):
+        s2 = by_side(role, third_c[:, :half], third_c[:, half:])
+        s3 = by_side(role, extra_c[:, :eighth], extra_c[:, eighth:])
+        return jnp.concatenate([s2, s3], axis=1)
+
+    c1_mine, c2_mine = pick(cotangent, side), second_cot(side)
+    c1_other = over(after(pick(cotangent, 1 - side), x1_other))
+    c2_other = over(after(second_cot(1 - side), x2_other))
+
+    places = shard * bins + jnp.arange(bins, dtype=jnp.int32)
+    valid_rows = (places[None, :] < lengths[:, None]).astype(jnp.float32)[:, None, :]
+    x_wide = inputs.astype(jnp.float32)
+    mine = (jnp.arange(2) == side).astype(jnp.float32)[:, None, None]
+    lead = ((shard == 0) & (group_at == 0)).astype(jnp.float32)
+    stats = jnp.stack(
+        [
+            jnp.sum(valid_rows * x_wide, axis=(0, 2)),
+            jnp.sum(valid_rows * x_wide * x_wide, axis=(0, 2)),
+            lead * gain_in,
+            lead * offset_in,
+        ]
+    )
+    stats, filled = lax.psum(
+        (mine * stats[None], 0.5 * jnp.sum(valid_rows)), axes
+    )
+    mean = stats[:, 0] / filled
+    scale = lax.rsqrt(stats[:, 1] / filled - mean * mean + EPS)
+    norm_all = jnp.stack([mean, scale, stats[:, 2], stats[:, 3]], axis=-1)
+    cols_mine = lax.dynamic_index_in_dim(norm_all, side, 0, keepdims=False)
+    cols_other = lax.dynamic_index_in_dim(norm_all, 1 - side, 0, keepdims=False)
+
+    starts = (
+        shard * bins,
+        shard * bins + side * half,
+        (shard % quarter) * bins + group * piece + side * eighth,
+    )
+    limits = (lax.dynamic_index_in_dim(ranked, side, 0, keepdims=False), ranked[2], ranked[3])
+    valid_ext, valid_own = [], []
+    for at, size, limit in zip(starts, (bins, half, eighth), limits, strict=True):
+        spots = at - LANES + jnp.arange(size + 2 * LANES, dtype=jnp.int32)
+        good = ((spots >= 0) & (spots < limit)).astype(jnp.float32)[None, :]
+        valid_ext.append(good)
+        valid_own.append(good[:, LANES : LANES + size])
+    valid_ext = jnp.concatenate(valid_ext, axis=1)
+    valid_own = jnp.concatenate(valid_own, axis=1)
+
+    def activate(first, second, cols):
+        h1, h2, h3 = (second[:, LANES * i : LANES * (i + 1)] for i in range(3))
+        s2, s3 = second[:, 3 * LANES : 3 * LANES + half], second[:, 3 * LANES + half :]
+        wide = jnp.concatenate([h1, first, h1, h2, s2, h2, h3, s3, h3], axis=1).astype(jnp.float32)
+        norm = (wide - cols[:, 0:1]) * cols[:, 1:2]
+        return (gelu(norm * cols[:, 2:3] + cols[:, 3:4]) * valid_ext).astype(jnp.bfloat16)
+
+    act_mine = activate(x1_mine, x2_mine, cols_mine)
+    act_other = activate(x1_other, x2_other, cols_other)
+
+    turn = lambda w: jnp.transpose(w, (2, 0, 1)).reshape(bottle, taps * chans)
+    conv_out, sum_first, sum_second = conv_forward(
+        act_mine,
+        act_other,
+        jnp.concatenate([turn(conv_weight), turn(conv_other)], axis=1),
+        valid_own,
+        tiles,
+    )
+    sum_first, sum_second = lax.psum(
+        (jnp.sum(sum_first, axis=1), jnp.sum(sum_second, axis=1)), axes
+    )
+    mean_mid = sum_first / filled
+    scale_mid = lax.rsqrt(sum_second / filled - mean_mid * mean_mid + EPS)
+    cols_mid = jnp.stack([mean_mid, scale_mid, gain_mid, offset_mid], axis=-1)
+
+    norm_mid = (conv_out - cols_mid[:, 0:1]) * cols_mid[:, 1:2]
+    act_mid = (gelu(norm_mid * cols_mid[:, 2:3] + cols_mid[:, 3:4]) * valid_own).astype(jnp.bfloat16)
+
+    point_all = jnp.concatenate([point_weight, point_other], axis=1)
+    grad1, beta1, gamma1, outer1 = mid_back(
+        conv_out, act_mid, valid_own, c1_mine, c1_other, point_all, cols_mid, 0
+    )
+    grad2, beta2, gamma2, outer2 = mid_back(
+        conv_out, act_mid, valid_own, c2_mine, c2_other, point_all, cols_mid, tiles[0]
+    )
+    grad_bias = jnp.sum(cotangent.astype(jnp.float32), axis=(0, 2))
+    beta_mid, gamma_mid, grad_bias = lax.psum(
+        (
+            jnp.sum(beta1 + beta2, axis=1),
+            jnp.sum(gamma1 + gamma2, axis=1),
+            mine[:, 0] * grad_bias[None],
+        ),
+        axes,
+    )
+    grad_bias = lax.dynamic_index_in_dim(grad_bias, side, 0, keepdims=False)
+    factor = (gain_mid * scale_mid)[:, None]
+
+    def conv_grad(grad, lo, hi):
+        kept = valid_own[:, lo:hi] * (beta_mid[:, None] + norm_mid[:, lo:hi] * gamma_mid[:, None])
+        return (factor * (grad - kept / filled)).astype(jnp.bfloat16)
+
+    low2 = conv_grad(grad2, bins, bins + half + eighth)
+    low1 = conv_grad(grad1, 0, bins)
+
+    act2_mine = after(act_mid[:, bins:], c1_other)
+    act2_other = over(act2_mine)
+    low2_other = over(after(low2, c2_other))
+    low1_other = over(after(low1, act2_other))
+    act1_mine = act_mid[:, :bins]
+    act1_other = over(after(act1_mine, low2_other))
+
+    grad_conv = conv_weight_back(act_mine, act_other, low1, low2, tiles)
+    outer = outer1 + outer2
+    depth = taps * chans
+    sums = jnp.stack(
+        [
+            jnp.concatenate([grad_conv[:depth], outer[:, :chans]], axis=0),
+            jnp.concatenate([grad_conv[depth:], outer[:, chans:]], axis=0),
+        ]
+    )
+    sums = lax.psum_scatter(sums, ("win", "seq"), scatter_dimension=1, tiled=True)
+    sums = lax.all_gather(sums[0] + over(sums[1]), ("win", "seq"), axis=0, tiled=True)
+    grad_conv = sums[:depth].reshape(taps, chans, bottle)
+    grad_point = sums[depth:]
+
+    weight_out = jnp.transpose(point_weight)
+    bias = point_bias[:, None]
+    pair_of = lambda cells_mine, cells_other: by_side(
+        side,
+        jnp.concatenate([cells_mine, cells_other], axis=1),
+        jnp.concatenate([cells_other, cells_mine], axis=1),
+    )
+    out_tile = 2 * TILE
+    at_slot = lambda slot, tile: jnp.stack(
+        [lax.dynamic_index_in_dim(order, slot, 0, keepdims=False), jnp.asarray(tile, jnp.int32)]
+    )
+    write = lambda prev, act, size, place: write_outputs(
+        prev, act, size // out_tile, place, inputs, weight_out, bias
+    )
+    half_tiles = half // out_tile
+    outputs = write(None, act1_mine, bins, at_slot(side, 0))
+    outputs = write(outputs, act2_mine, half, at_slot(2, side * half_tiles))
+    outputs = write(outputs, act2_other, half, at_slot(2, (1 - side) * half_tiles))
+    act_quarter = collect(pair_of(act2_mine[:, half:], act2_other[:, half:]))
+    outputs = write(outputs, act_quarter, bins, at_slot(3, 0))
+    outputs = write(outputs, act1_other, bins, at_slot(1 - side, 0))
+
+    low_quarter = collect(pair_of(low2[:, half:], low2_other[:, half:]))
+    low_third = pair_of(low2[:, :half], low2_other[:, :half])
+    slots = jnp.stack(
+        [by_side(side, low1, low1_other), by_side(side, low1_other, low1), low_third, low_quarter]
+    )
+    edges = jnp.concatenate([slots[..., :LANES], slots[..., -LANES:]], axis=2)
+    right = lax.ppermute(edges[..., :LANES], "seq", back_ends)
+    left = lax.ppermute(edges[..., LANES:], "seq", ends)
+    border = jnp.where(low_lanes, right, left)
+    slots = jnp.concatenate([border, slots, border], axis=2)
+    valid_slots = (places[None, :] < ranked[:, None]).astype(jnp.float32)[:, None, :]
+    weight_back = jnp.transpose(conv_weight, (1, 0, 2)).reshape(chans, taps * bottle)
+    grad_in, beta_in, gamma_in = input_back(
+        order, slots, inputs, valid_slots, weight_back, cols_mine
+    )
+    beta_in, gamma_in = lax.psum(
+        (jnp.sum(beta_in, axis=1), jnp.sum(gamma_in, axis=1)), ("seq", "win")
+    )
+    norm_in = (x_wide - cols_mine[:, 0:1]) * cols_mine[:, 1:2]
+    factor_in = (cols_mine[:, 2] * cols_mine[:, 1])[:, None]
+    grad_inputs = (
+        cotangent.astype(jnp.float32)
+        + factor_in
+        * (grad_in - valid_rows * (column(beta_in) + norm_in * column(gamma_in)) / filled)
+    ).astype(jnp.bfloat16)
+    part = bottle // 2
+    return (
+        outputs,
+        grad_inputs,
+        gamma_in,
+        beta_in,
+        grad_conv,
+        lax.dynamic_slice_in_dim(gamma_mid, side * part, part),
+        lax.dynamic_slice_in_dim(beta_mid, side * part, part),
+        grad_point,
+        grad_bias,
+    )
+
+
 def solution(mesh):
+    two_groups = mesh.shape["ch"] == 2 and mesh.shape["seq"] % 4 == 0
+
+    def local(*args):
+        windows, _, bins = args[0].shape
+        if two_groups and windows == 4 and bins % (8 * TILE) == 0:
+            return local_pair(*args)
+        return local_any(*args)
+
     return jax.shard_map(
         local,
         mesh=mesh,

time: 1550 us -> 785 us (0.51)
  waiting for transfers between devices: 955 us -> 167 us
  matrix products: 194 us -> 0 us
  Pallas kernels: 0 us -> 142 us
  local copies, waits for them, and re-layouts: 160 us -> 60.2 us
  blocking collectives: 134 us -> 196 us
  other arithmetic: 80.8 us -> 129 us
  starting transfers between devices: 7.64 us -> 53.1 us
    unnamed x5 -> x3, waiting for transfers between devices: 826 us -> 0.05 us
    dot_general x6 -> x0, matrix products: 194 us -> none  [the longest x1 57 us: local(): jnp.einsum('wkt,kc->wct', back_taps, back_weight, preferred_element_type=...]
    ppermute x4 -> x26, waiting for transfers between devices: 0.01 us -> 167 us  [the longest x6 67.8 us: collect(): lax.ppermute(cells, 'seq', [(i + k * quarter, i) for i in range(quarter)])]
    pallas_call x0 -> x10, Pallas kernels: none -> 142 us  [the longest x1 42.1 us: input_back(): pl.pallas_call(back_kernel, grid_spec=pltpu.PrefetchScalarGridSpec(num_sc...]
    all_gather x2, waiting for transfers between devices: 129 us -> 0.02 us  [the longest x1 0.02 us: local_pair(): lax.all_gather(sums[0] + over(sums[1]), ('win', 'seq'), axis=0, tiled=True)]
    psum x4, blocking collectives: 134 us -> 196 us  [the longest x1 75.4 us: local_pair(): lax.psum((mine * stats[None], 0.5 * jnp.sum(valid_rows)), axes)]
    unnamed x55 -> x120, local copies, waits for them, and re-layouts: 76.6 us -> 15.7 us
    transpose x2 -> x0, local copies, waits for them, and re-layouts: 51.1 us -> none  [the longest x1 28.4 us: local(): jnp.einsum('wct,fc->wft', cotangent, point_weight, preferred_element_type...]
  transfers between devices with their start and end apart: 8 -> 29, of which waited for: 3 -> 9; matrix products, arithmetic and copies ran while one was open for 18% -> 21% of each run, Pallas kernels for 0% -> 14%
where the time goes in v1:
time: 785 us; the launch traced here: 774 us
  blocking collectives  196 us (25%)
  waiting for transfers between devices  167 us (21%)
  Pallas kernels  142 us (18%)
  other arithmetic  129 us (16%)
  local copies, waits for them, and re-layouts  60.2 us (8%)
  starting transfers between devices  53.1 us (7%)
  between operations  27.1 us (3%)
    psum x1, blocking collectives, local_pair(): lax.psum((mine * stats[None], 0.5 * jnp.sum(valid_rows)), axes)  75.4 us
    ppermute x6, waiting for transfers between devices, collect(): lax.ppermute(cells, 'seq', [(i + k * quarter, i) for i in range(quarter)])  67.8 us
    ppermute x10, waiting for transfers between devices, local_pair(): over = lambda cells: lax.ppermute(cells, 'ch', swap)  58.1 us
    psum x1, blocking collectives, local_pair(): lax.psum((jnp.sum(beta1 + beta2, axis=1), jnp.sum(gamma1 + gamma2, axis=1...  48.6 us
    pallas_call x1, Pallas kernels, input_back(): pl.pallas_call(back_kernel, grid_spec=pltpu.PrefetchScalarGridSpec(num_sc...  42.1 us
    psum x1, blocking collectives, local_pair(): lax.psum((jnp.sum(sum_first, axis=1), jnp.sum(sum_second, axis=1)), axes)  41.1 us
    ppermute x6, waiting for transfers between devices, spread(): lax.ppermute(parts[k], 'seq', [(i, i + k * quarter) for i in range(quarte...  41 us
    psum x1, blocking collectives, local_pair(): lax.psum((jnp.sum(beta_in, axis=1), jnp.sum(gamma_in, axis=1)), ('seq', '...  31.1 us
  transfers between devices with their start and end apart: 29, of which 9 were waited for; matrix products, arithmetic and copies ran while one was open for 21% of the time, Pallas kernels for 14%

profile of v1, /device:TPU:0, one launch (start us, length us, event | category | flops | bytes accessed | tf_op | source)
XLA Modules:
  0.0 774.4 jit_solution(8673165018048721829)
XLA Ops:
  22.2 6.1 dynamic-slice_bitcast_fusion.3
  34.2 8.3 %fusion = (f32[384]{0:T(512)S(1)}, f32[384]{0:T(512)S(1)}) fusion(bf16[4,384,3072]{2,1,0:T(8,128)(2,1)} %x.11, f32[4,3072]{1,0:T(4,128)S(1)} %compare_convert_fusion.1), kind=kLoop, calls=%fused_computation.3 | loop fusion | flops 23592192 | bytes 9489408 | tf_op jit(solution)/shard_map/reduce_sum | solution.py:576
  43.3 75.4 %all-reduce.2 = (f32[2,4,384]{2,0,1:T(2,128)S(1)}, f32[]{:T(128)}) all-reduce(f32[2,4,384]{2,0,1:T(2,128)S(1)} %broadcast_multiply_fusion, f32[]{:T(128)S(6)} %mul.383), channel_id=1, replica_groups=mesh['seq'=8,'ch'=2,'win'=2] {'seq','ch','win'}, use_global_device_ids=true, to_apply=%region_4.5 | all-reduce | flops 3073 | bytes 24584 | tf_op jit(solution)/shard_map/psum | solution.py:582
  158.7 17.1 %collective-permute-done.3 = bf16[384,896]{1,0:T(8,128)(2,1)} collective-permute-done((bf16[384,896]{1,0:T(8,128)(2,1)}, bf16[384,896]{1,0:T(8,128)(2,1)}, u32[]{:S(2)}, u32[]{:S(2)}) %collective-permute-start.3) | collective-permute-done | bytes 688160 | tf_op jit(solution)/shard_map/ppermute | solution.py:516
  175.8 18.0 %collective-permute-done.4 = bf16[384,896]{1,0:T(8,128)(2,1)} collective-permute-done((bf16[384,896]{1,0:T(8,128)(2,1)}, bf16[384,896]{1,0:T(8,128)(2,1)}, u32[]{:S(2)}, u32[]{:S(2)}) %collective-permute-start.4) | collective-permute-done | bytes 688160 | tf_op jit(solution)/shard_map/ppermute | solution.py:516
  216.5 7.1 collective-permute-start.10
  229.4 13.0 %collective-permute-done.5 = bf16[384,2304]{1,0:T(8,128)(2,1)} collective-permute-done((bf16[384,2304]{1,0:T(8,128)(2,1)}, bf16[384,2304]{1,0:T(8,128)(2,1)}, u32[]{:S(2)}, u32[]{:S(2)}) %collective-permute-start.5) | collective-permute-done | bytes 1769504 | tf_op jit(solution)/shard_map/ppermute | solution.py:474
  250.8 11.0 %fusion.25 = (bf16[384,5760]{1,0:T(8,128)(2,1)}, bf16[384,5760]{1,0:T(8,128)(2,1)}) fusion(bf16[384,5760]{1,0:T(8,128)(2,1)S(1)} %slice_dynamic-update-slice_fusion.4, f32[384]{0:T(512)S(1)} %get-tuple-element.44, f32[384]{0:T(512)S(1)} %get-tuple-element.45, f32[384]{0:T(512)S(1)} %get-tuple-element.46, f32[384]{0:T(512)S(1)} %get-tuple-element.43, ...), kind=kLoop, calls=%fused_computation.34 | loop fusion | flops 66355200 | bytes 17730048 | tf_op jit(solution)/shard_map/convert_element_type | solution.py:611
  261.7 22.2 %shard_map.169 = (f32[384,4992]{1,0:T(8,128)}, f32[384,128]{1,0:T(8,128)S(1)}, f32[384,128]{1,0:T(8,128)S(1)}) custom-call(bf16[384,5760]{1,0:T(8,128)(2,1)} %get-tuple-element.124.own, bf16[384,5760]{1,0:T(8,128)(2,1)} %get-tuple-element.123.other, bf16[384,2304]{1,0:T(8,128)(2,1)S(1)} %pad_maximum_fusion.3.weight, f32[1,4992]{1,0:T(1,128)S(1)} %copy-done.2), custom_call_target="tpu_custom_call" | custom-call | flops 8833204224 | bytes 16515072 | tf_op jit(solution)/shard_map/pallas_call | solution.py:245
  284.8 41.1 %all-reduce.1 = (f32[384]{0:T(512)S(1)}, f32[384]{0:T(512)S(1)}) all-reduce(f32[384]{0:T(512)S(1)} %reduce_sum.124, f32[384]{0:T(512)} %reduce_sum.123), channel_id=1, replica_groups=mesh['seq'=8,'ch'=2,'win'=2] {'seq','ch','win'}, use_global_device_ids=true, to_apply=%region_11.12 | all-reduce | flops 768 | bytes 6144 | tf_op jit(solution)/shard_map/psum | solution.py:624
  334.5 8.7 %fusion.33 = (bf16[384,4992]{1,0:T(8,128)(2,1)}, f32[384,4992]{1,0:T(8,128)}) fusion(f32[4992]{0:T(1024)S(1)} %copy-done.25, f32[384]{0:T(512)S(1)} %copy-done.39, f32[384]{0:T(512)S(1)} %copy-done.28, f32[384]{0:T(512)S(1)} %get-tuple-element.67, f32[384,4992]{1,0:T(8,128)} %get-tuple-element.23.conv, f32[384]{0:T(512)S(1)} %get-tuple-element.129), kind=kLoop, calls=%fused_computation.42 | loop fusion | flops 26836992 | bytes 19195392 | tf_op jit(solution)/shard_map/convert_element_type | solution.py:632
  343.3 22.1 %collective-permute-done.11.other = bf16[384,1920]{1,0:T(8,128)(2,1)S(1)} collective-permute-done((bf16[384,1920]{1,0:T(8,128)(2,1)S(1)}, bf16[384,1920]{1,0:T(8,128)(2,1)S(1)}, u32[]{:S(2)}, u32[]{:S(2)}) %collective-permute-start.11) | collective-permute-done | bytes 1474592 | tf_op jit(solution)/shard_map/ppermute | solution.py:474
  366.6 9.8 %shard_map.170 = (f32[384,1920]{1,0:T(8,128)}, f32[384,128]{1,0:T(8,128)S(1)}, f32[384,128]{1,0:T(8,128)S(1)}, f32[384,768]{1,0:T(8,128)S(1)}) custom-call(f32[384,4992]{1,0:T(8,128)} %get-tuple-element.23.conv, bf16[384,4992]{1,0:T(8,128)(2,1)} %get-tuple-element.68.act, f32[1,4992]{1,0:T(1,128)S(1)} %copy-done.3, ...), custom_call_target="tpu_custom_call" | custom-call | flops 2264924160 | bytes 10321920 | tf_op jit(solution)/shard_map/pallas_call | solution.py:296
  382.2 14.1 %shard_map.171 = (f32[384,3072]{1,0:T(8,128)}, f32[384,128]{1,0:T(8,128)S(1)}, f32[384,128]{1,0:T(8,128)S(1)}, f32[384,768]{1,0:T(8,128)S(1)}) custom-call(f32[384,4992]{1,0:T(8,128)} %get-tuple-element.23.conv, bf16[384,4992]{1,0:T(8,128)(2,1)} %get-tuple-element.68.act, f32[1,4992]{1,0:T(1,128)S(1)} %copy-done.3, ...), custom_call_target="tpu_custom_call" | custom-call | flops 3623878656 | bytes 16515072 | tf_op jit(solution)/shard_map/pallas_call | solution.py:296
  397.0 48.6 %all-reduce = (f32[384]{0:T(512)S(1)}, f32[384]{0:T(512)S(1)}, f32[2,384]{1,0:T(2,128)S(1)}) all-reduce(f32[384]{0:T(512)S(1)} %add_reduce_fusion, f32[384]{0:T(512)S(1)} %add_reduce_fusion.1, f32[2,384]{1,0:T(2,128)S(1)} %copy-done.35), channel_id=1, replica_groups=mesh['seq'=8,'ch'=2,'win'=2] {'seq','ch','win'}, use_global_device_ids=true, to_apply=%region_15.16 | all-reduce | flops 1536 | bytes 12288 | tf_op jit(solution)/shard_map/psum | solution.py:642
  445.7 6.7 broadcast_add_fusion.2
  459.5 30.0 %shard_map.178 = f32[2304,384]{1,0:T(8,128)} custom-call(bf16[384,5760]{1,0:T(8,128)(2,1)} %get-tuple-element.124.own, bf16[384,5760]{1,0:T(8,128)(2,1)} %get-tuple-element.123.other, bf16[384,3072]{1,0:T(8,128)(2,1)S(1)} %get-tuple-element.59.near, bf16[384,1920]{1,0:T(8,128)(2,1)S(1)} %get-tuple-element.65.far), custom_call_target="tpu_custom_call" | custom-call | flops 8833204224 | bytes 8847360 | tf_op jit(solution)/shard_map/pallas_call | solution.py:347
  511.5 18.3 %collective-permute-done.13 = bf16[384,1920]{1,0:T(8,128)(2,1)} collective-permute-done((bf16[384,1920]{1,0:T(8,128)(2,1)}, bf16[384,1920]{1,0:T(8,128)(2,1)}, u32[]{:S(2)}, u32[]{:S(2)}) %collective-permute-start.13) | collective-permute-done | bytes 1474592 | tf_op jit(solution)/shard_map/ppermute | solution.py:474
  544.8 41.7 %collective-permute-done.20 = bf16[384,768]{1,0:T(8,128)(2,1)S(1)} collective-permute-done((bf16[384,768]{1,0:T(8,128)(2,1)S(1)}, bf16[384,768]{1,0:T(8,128)(2,1)S(1)}, u32[]{:S(2)}, u32[]{:S(2)}) %collective-permute-start.20) | collective-permute-done | bytes 589856 | tf_op jit(solution)/shard_map/ppermute | solution.py:522
  605.5 26.1 %collective-permute-done.16 = bf16[384,768]{1,0:T(8,128)(2,1)} collective-permute-done((bf16[384,768]{1,0:T(8,128)(2,1)}, bf16[384,768]{1,0:T(8,128)(2,1)}, u32[]{:S(2)}, u32[]{:S(2)}) %collective-permute-start.16) | collective-permute-done | bytes 589856 | tf_op jit(solution)/shard_map/ppermute | solution.py:522
  661.5 8.8 %pad_maximum_fusion.grads = bf16[4,384,3328]{2,1,0:T(8,128)(2,1)} fusion(bf16[4,384,128]{2,1,0:T(8,128)(2,1)S(1)} %broadcast_select_fusion.4, bf16[1,384,3072]{2,1,0:T(8,128)(2,1)} %copy-done.8, bf16[1,384,3072]{2,1,0:T(8,128)(2,1)} %copy-done.7, bf16[1,384,3072]{2,1,0:T(8,128)(2,1)} %copy-done.10, bf16[1,384,3072]{2,1,0:T(8,128)(2,1)} %copy-done.9), kind=kLoop, calls=%fused_computation.18 | loop fusion | flops 61341696 | bytes 20054016 | tf_op jit(solution)/shard_map/concatenate | solution.py:712
  670.4 42.1 %shard_map.177 = (f32[4,384,3072]{2,1,0:T(8,128)}, f32[384,128]{1,0:T(8,128)S(1)}, f32[384,128]{1,0:T(8,128)S(1)}) custom-call(s32[4]{0:T(128)S(1)} %copy-done.5, bf16[4,384,3328]{2,1,0:T(8,128)(2,1)} %pad_maximum_fusion.grads, bf16[4,384,3072]{2,1,0:T(8,128)(2,1)} %x.11, f32[4,1,3072]{2,1,0:T(1,128)S(1)} %compare_convert_fusion.valid, ...), custom_call_target="tpu_custom_call" | custom-call | flops 10871635968 | bytes 28311552 | tf_op jit(solution)/shard_map/pallas_call | solution.py:423
  712.7 31.1 %all-reduce.3 = (f32[384]{0:T(512)S(1)}, f32[384]{0:T(512)S(1)}) all-reduce(f32[384]{0:T(512)S(1)} %reduce_sum.128, f32[384]{0:T(512)S(1)} %reduce_sum.127), channel_id=1, replica_groups=mesh['seq'=8,'ch'=2,'win'=2] {'seq','win'}, use_global_device_ids=true, to_apply=%region_19.20 | all-reduce | flops 768 | bytes 6144 | tf_op jit(solution)/shard_map/psum | solution.py:718
  743.8 19.1 %fusion.1 = bf16[4,384,3072]{2,1,0:T(8,128)(2,1)} fusion(bf16[4,384,3072]{2,1,0:T(8,128)(2,1)} %param.19, f32[4,384,3072]{2,1,0:T(8,128)} %get-tuple-element.32, bf16[4,384,3072]{2,1,0:T(8,128)(2,1)} %x.11, f32[]{:T(128)} %get-tuple-element.55, f32[384]{0:T(512)S(1)} %get-tuple-element.56, f32[384]{0:T(512)S(1)} %get-tuple-element.42, f32[384]{0:T(512)S(1)} %copy-done.30, ...), kind=kLoop, calls=%fused_computation.6 | loop fusion | flops 56623104 | bytes 47242756 | tf_op jit(solution)/shard_map/convert_element_type | solution.py:727
  (302 shorter events, 200.9 us)
Async XLA Ops:
  7.2 195.3 %all-gather.3.cloned.1.call-start = ((), (), s32[]{:S(2)}) async-start(), calls=%async_computation.1 | async-start | bytes 1253376 | tf_op jit(solution)/shard_map/all_gather | solution.py:494
  9.3 123.7 %collective-permute-start = (bf16[4,384,128]{2,1,0:T(8,128)(2,1)}, bf16[4,384,128]{2,1,0:T(8,128)(2,1)}, u32[]{:S(2)}, u32[]{:S(2)}) collective-permute-start(bf16[4,384,128]{2,1,0:T(8,128)(2,1)} %get-tuple-element.90), channel_id=1, source_target_pairs={{4,0},{8,4},{12,8},{16,12},{20,16},{24,20},{28,24},{5,1},{9,5},{13... | collective-permute-start | bytes 1179656 | tf_op jit(solution)/shard_map/ppermute | solution.py:507
  10.6 122.4 %collective-permute-start.1 = (bf16[4,384,128]{2,1,0:T(8,128)(2,1)}, bf16[4,384,128]{2,1,0:T(8,128)(2,1)}, u32[]{:S(2)}, u32[]{:S(2)}) collective-permute-start(bf16[4,384,128]{2,1,0:T(8,128)(2,1)} %get-tuple-element.89), channel_id=1, source_target_pairs={{0,4},{4,8},{8,12},{12,16},{16,20},{20,24},{24,28},{1,5},{5,9},{9,... | collective-permute-start | bytes 1179656 | tf_op jit(solution)/shard_map/ppermute | solution.py:508
  28.3 178.4 %collective-permute-start.6 = (bf16[384,3072]{1,0:T(8,128)(2,1)}, bf16[384,3072]{1,0:T(8,128)(2,1)}, u32[]{:S(2)}, u32[]{:S(2)}) collective-permute-start(bf16[384,3072]{1,0:T(8,128)(2,1)} %get-tuple-element.86), channel_id=1, source_target_pairs={{0,2},{2,0},{1,3},{3,1},{4,6},{6,4},{5,7},{7,5},{8,10},{10,8},{9,1... | collective-permute-start | bytes 7077896 | tf_op jit(solution)/shard_map/ppermute | solution.py:474
  32.0 119.9 %collective-permute-start.7 = (bf16[96,384]{1,0:T(8,128)(2,1)}, bf16[96,384]{1,0:T(8,128)(2,1)}, u32[]{:S(2)}, u32[]{:S(2)}) collective-permute-start(bf16[96,384]{1,0:T(8,128)(2,1)} %fusion.53), channel_id=1, source_target_pairs={{0,2},{2,0},{1,3},{3,1},{4,6},{6,4},{5,7},{7,5},{8,10},{10,8},{9,1... | collective-permute-start | bytes 221192 | tf_op jit(solution)/shard_map/ppermute | solution.py:474
  147.6 46.2 %collective-permute-start.4 = (bf16[384,896]{1,0:T(8,128)(2,1)}, bf16[384,896]{1,0:T(8,128)(2,1)}, u32[]{:S(2)}, u32[]{:S(2)}) collective-permute-start(bf16[384,896]{1,0:T(8,128)(2,1)} %pad_maximum_fusion.7), channel_id=1, source_target_pairs={{0,24},{4,28},{1,25},{5,29},{2,26},{6,30},{3,27},{7,31}} | collective-permute-start | bytes 2064392 | tf_op jit(solution)/shard_map/ppermute | solution.py:516
  151.9 500.8 %reduce-scatter.2.cloned.1.call-start = ((), (), s32[]{:S(2)}) async-start(), calls=%async_computation.2 | async-start | bytes 5013504 | tf_op jit(solution)/shard_map/reduce_scatter | solution.py:676
  200.5 41.9 %collective-permute-start.5 = (bf16[384,2304]{1,0:T(8,128)(2,1)}, bf16[384,2304]{1,0:T(8,128)(2,1)}, u32[]{:S(2)}, u32[]{:S(2)}) collective-permute-start(bf16[384,2304]{1,0:T(8,128)(2,1)} %get-tuple-element.115), channel_id=1, source_target_pairs={{0,2},{2,0},{1,3},{3,1},{4,6},{6,4},{5,7},{7,5},{8,10},{10,8},{9,1... | collective-permute-start | bytes 5308424 | tf_op jit(solution)/shard_map/ppermute | solution.py:474
  214.5 161.9 %collective-permute-start.12 = (bf16[384,3072]{1,0:T(8,128)(2,1)}, bf16[384,3072]{1,0:T(8,128)(2,1)}, u32[]{:S(2)}, u32[]{:S(2)}) collective-permute-start(bf16[384,3072]{1,0:T(8,128)(2,1)} %get-tuple-element.82), channel_id=1, source_target_pairs={{0,2},{2,0},{1,3},{3,1},{4,6},{6,4},{5,7},{7,5},{8,10},{10,8},{9,1... | collective-permute-start | bytes 7077896 | tf_op jit(solution)/shard_map/ppermute | solution.py:474
  216.5 113.5 %collective-permute-start.10 = (bf16[384,768]{1,0:T(8,128)(2,1)}, bf16[384,768]{1,0:T(8,128)(2,1)}, u32[]{:S(2)}, u32[]{:S(2)}) collective-permute-start(bf16[384,768]{1,0:T(8,128)(2,1)} %get-tuple-element.110), channel_id=1, source_target_pairs={{0,24},{4,28},{1,25},{5,29},{2,26},{6,30},{3,27},{7,31}} | collective-permute-start | bytes 1769480 | tf_op jit(solution)/shard_map/ppermute | solution.py:516
  223.6 106.5 %collective-permute-start.8 = (bf16[384,768]{1,0:T(8,128)(2,1)}, bf16[384,768]{1,0:T(8,128)(2,1)}, u32[]{:S(2)}, u32[]{:S(2)}) collective-permute-start(bf16[384,768]{1,0:T(8,128)(2,1)} %get-tuple-element.109), channel_id=1, source_target_pairs={{0,8},{4,12},{1,9},{5,13},{2,10},{6,14},{3,11},{7,15}} | collective-permute-start | bytes 1769480 | tf_op jit(solution)/shard_map/ppermute | solution.py:516
  225.7 104.4 %collective-permute-start.9 = (bf16[384,768]{1,0:T(8,128)(2,1)}, bf16[384,768]{1,0:T(8,128)(2,1)}, u32[]{:S(2)}, u32[]{:S(2)}) collective-permute-start(bf16[384,768]{1,0:T(8,128)(2,1)} %get-tuple-element.111), channel_id=1, source_target_pairs={{0,16},{4,20},{1,17},{5,21},{2,18},{6,22},{3,19},{7,23}} | collective-permute-start | bytes 1769480 | tf_op jit(solution)/shard_map/ppermute | solution.py:516
  332.1 33.3 %collective-permute-start.11 = (bf16[384,1920]{1,0:T(8,128)(2,1)S(1)}, bf16[384,1920]{1,0:T(8,128)(2,1)S(1)}, u32[]{:S(2)}, u32[]{:S(2)}) collective-permute-start(bf16[384,1920]{1,0:T(8,128)(2,1)S(1)} %maximum_add_fusion), channel_id=1, source_target_pairs={{0,2},{2,0},{1,3},{3,1},{4,6},{6,4},{5,7},{7,5},{8,10},{10,8},{9,1... | collective-permute-start | bytes 4423688 | tf_op jit(solution)/shard_map/ppermute | solution.py:474
  380.9 71.5 %collective-permute-start.15 = (bf16[384,1920]{1,0:T(8,128)(2,1)}, bf16[384,1920]{1,0:T(8,128)(2,1)}, u32[]{:S(2)}, u32[]{:S(2)}) collective-permute-start(bf16[384,1920]{1,0:T(8,128)(2,1)} %slice_add_fusion.act), channel_id=1, source_target_pairs={{0,2},{2,0},{1,3},{3,1},{4,6},{6,4},{5,7},{7,5},{8,10},{10,8},{9,1... | collective-permute-start | bytes 4423688 | tf_op jit(solution)/shard_map/ppermute | solution.py:474
  494.6 268.3 %all-gather.5.cloned.1.call-start = ((), (), s32[]{:S(2)}) async-start(), calls=%async_computation.3 | async-start | bytes 2506752 | tf_op jit(solution)/shard_map/all_gather | solution.py:677
  496.2 33.6 %collective-permute-start.13 = (bf16[384,1920]{1,0:T(8,128)(2,1)}, bf16[384,1920]{1,0:T(8,128)(2,1)}, u32[]{:S(2)}, u32[]{:S(2)}) collective-permute-start(bf16[384,1920]{1,0:T(8,128)(2,1)} %get-tuple-element.64), channel_id=1, source_target_pairs={{0,2},{2,0},{1,3},{3,1},{4,6},{6,4},{5,7},{7,5},{8,10},{10,8},{9,1... | collective-permute-start | bytes 4423688 | tf_op jit(solution)/shard_map/ppermute | solution.py:474
  530.9 55.5 %collective-permute-start.20 = (bf16[384,768]{1,0:T(8,128)(2,1)S(1)}, bf16[384,768]{1,0:T(8,128)(2,1)S(1)}, u32[]{:S(2)}, u32[]{:S(2)}) collective-permute-start(bf16[384,768]{1,0:T(8,128)(2,1)S(1)} %get-tuple-element.61), channel_id=1, source_target_pairs={{8,0},{12,4},{9,1},{13,5},{10,2},{14,6},{11,3},{15,7}} | collective-permute-start | bytes 1769480 | tf_op jit(solution)/shard_map/ppermute | solution.py:522
  532.2 55.5 %collective-permute-start.21 = (bf16[384,768]{1,0:T(8,128)(2,1)S(1)}, bf16[384,768]{1,0:T(8,128)(2,1)S(1)}, u32[]{:S(2)}, u32[]{:S(2)}) collective-permute-start(bf16[384,768]{1,0:T(8,128)(2,1)S(1)} %get-tuple-element.61), channel_id=1, source_target_pairs={{16,0},{20,4},{17,1},{21,5},{18,2},{22,6},{19,3},{23,7}} | collective-permute-start | bytes 1769480 | tf_op jit(solution)/shard_map/ppermute | solution.py:522
  533.5 55.7 %collective-permute-start.22 = (bf16[384,768]{1,0:T(8,128)(2,1)S(1)}, bf16[384,768]{1,0:T(8,128)(2,1)S(1)}, u32[]{:S(2)}, u32[]{:S(2)}) collective-permute-start(bf16[384,768]{1,0:T(8,128)(2,1)S(1)} %get-tuple-element.61), channel_id=1, source_target_pairs={{24,0},{28,4},{25,1},{29,5},{26,2},{30,6},{27,3},{31,7}} | collective-permute-start | bytes 1769480 | tf_op jit(solution)/shard_map/ppermute | solution.py:522
  534.8 98.5 %collective-permute-start.19 = (bf16[384,3072]{1,0:T(8,128)(2,1)}, bf16[384,3072]{1,0:T(8,128)(2,1)}, u32[]{:S(2)}, u32[]{:S(2)}) collective-permute-start(bf16[384,3072]{1,0:T(8,128)(2,1)} %get-tuple-element.58), channel_id=1, source_target_pairs={{0,2},{2,0},{1,3},{3,1},{4,6},{6,4},{5,7},{7,5},{8,10},{10,8},{9,1... | collective-permute-start | bytes 7077896 | tf_op jit(solution)/shard_map/ppermute | solution.py:474
  542.1 89.5 %collective-permute-start.16 = (bf16[384,768]{1,0:T(8,128)(2,1)}, bf16[384,768]{1,0:T(8,128)(2,1)}, u32[]{:S(2)}, u32[]{:S(2)}) collective-permute-start(bf16[384,768]{1,0:T(8,128)(2,1)} %get-tuple-element.63), channel_id=1, source_target_pairs={{8,0},{12,4},{9,1},{13,5},{10,2},{14,6},{11,3},{15,7}} | collective-permute-start | bytes 1769480 | tf_op jit(solution)/shard_map/ppermute | solution.py:522
  586.4 45.2 %collective-permute-start.17 = (bf16[384,768]{1,0:T(8,128)(2,1)}, bf16[384,768]{1,0:T(8,128)(2,1)}, u32[]{:S(2)}, u32[]{:S(2)}) collective-permute-start(bf16[384,768]{1,0:T(8,128)(2,1)} %get-tuple-element.63), channel_id=1, source_target_pairs={{16,0},{20,4},{17,1},{21,5},{18,2},{22,6},{19,3},{23,7}} | collective-permute-start | bytes 1769480 | tf_op jit(solution)/shard_map/ppermute | solution.py:522
  587.7 43.9 %collective-permute-start.18 = (bf16[384,768]{1,0:T(8,128)(2,1)}, bf16[384,768]{1,0:T(8,128)(2,1)}, u32[]{:S(2)}, u32[]{:S(2)}) collective-permute-start(bf16[384,768]{1,0:T(8,128)(2,1)} %get-tuple-element.63), channel_id=1, source_target_pairs={{24,0},{28,4},{25,1},{29,5},{26,2},{30,6},{27,3},{31,7}} | collective-permute-start | bytes 1769480 | tf_op jit(solution)/shard_map/ppermute | solution.py:522
  590.1 57.2 %collective-permute-start.14 = (bf16[384,3072]{1,0:T(8,128)(2,1)}, bf16[384,3072]{1,0:T(8,128)(2,1)S(1)}, u32[]{:S(2)}, u32[]{:S(2)}) collective-permute-start(bf16[384,3072]{1,0:T(8,128)(2,1)} %get-tuple-element.94), channel_id=1, source_target_pairs={{0,2},{2,0},{1,3},{3,1},{4,6},{6,4},{5,7},{7,5},{8,10},{10,8},{9,1... | collective-permute-start | bytes 7077896 | tf_op jit(solution)/shard_map/ppermute | solution.py:474
  (59 other events, 1440.2 us)
Sparse Core Ops, SparseCore 0:
  152.0 39.2 all-gather.2
  494.8 130.1 reduce-scatter.1
  661.6 40.5 all-gather.4

commit v2 on v0

--- a/solution.py
+++ b/solution.py
@@ -1,12 +1,17 @@
 import jax
 import jax.numpy as jnp
 from jax import lax
+from jax.experimental import pallas as pl
+from jax.experimental.pallas import tpu as pltpu
 from jax.sharding import PartitionSpec as P
 
 DILATION_BINS = 57
 
 
 EPS = 1e-05
+LANES = 128
+TILE = 384
+VMEM_BYTES = 63 * 1000 * 1000
 
 
 def with_halo(cells, sides, width):
@@ -34,7 +39,7 @@
     return vector[:, None]
 
 
-def local(
+def local_any(
     inputs,
     lengths,
     gain_in,
@@ -161,7 +166,1233 @@
     )
 
 
+MESH = pl.DeviceIdType.MESH
+ROWS = 32
+PLANE = 16
+F32 = jnp.float32
+BF16 = jnp.bfloat16
+GELU_A = 0.7978845608028654
+GELU_B = 0.044715
+
+
+def dot(a, b):
+    return jnp.dot(a, b, preferred_element_type=F32)
+
+
+def dot_t(a, b):
+    return lax.dot_general(a, b, (((1,), (1,)), ((), ())), preferred_element_type=F32)
+
+
+def lane_sum(cells):
+    total = cells[:, :LANES]
+    for at in range(LANES, cells.shape[1], LANES):
+        total = total + cells[:, at : at + LANES]
+    return total
+
+
+def gelu(v):
+    return 0.5 * v * (1.0 + jnp.tanh(GELU_A * (v + GELU_B * (v * v * v))))
+
+
+def gelu_slope(v):
+    square = v * v
+    th = jnp.tanh(GELU_A * (v + GELU_B * (v * square)))
+    return 0.5 * (1.0 + th) + 0.5 * v * (1.0 - th * th) * (GELU_A * (1.0 + 3.0 * GELU_B * square))
+
+
+def lanes_at(at, size):
+    return pl.ds(pl.multiple_of(at, LANES), size)
+
+
+def by_rows(count, body):
+    def step(i, carry):
+        body(pl.ds(pl.multiple_of(i * ROWS, ROWS), ROWS))
+        return carry
+
+    lax.fori_loop(0, count // ROWS, step, 0)
+
+
+def times(count, body):
+    def step(i, carry):
+        body(i)
+        return carry
+
+    lax.fori_loop(0, count, step, 0)
+
+
+def spread_lanes(cells, size):
+    return jnp.concatenate([cells] * (size // LANES), axis=1)
+
+
+def to_column(row):
+    return jnp.transpose(jnp.broadcast_to(row, (LANES, row.shape[1])))
+
+
+def to_row(cells):
+    return jnp.sum(jnp.transpose(cells), axis=0, keepdims=True)
+
+
+class Copies:
+    def __init__(self, send, recv):
+        self.send, self.recv, self.used = send, recv, 0
+
+    def take(self, count=1):
+        self.used += count
+        return self.used - count
+
+    def remote(self, src, dst, device, send_at=None, recv_at=None):
+        if send_at is None:
+            send_at = self.take()
+        if recv_at is None:
+            recv_at = send_at
+        return pltpu.make_async_remote_copy(
+            src_ref=src,
+            dst_ref=dst,
+            send_sem=self.send.at[send_at],
+            recv_sem=self.recv.at[recv_at],
+            device_id=device,
+            device_id_type=MESH,
+        )
+
+    def local(self, src, dst):
+        return pltpu.make_async_copy(src, dst, self.send.at[self.take()])
+
+
+class Place:
+    def __init__(self):
+        self.side, self.shard, self.win = (lax.axis_index(n) for n in ("ch", "seq", "win"))
+        self.group, self.core = self.shard // 2, self.shard % 2
+        self.me = self.win * 8 + self.shard
+        self.partner = {"ch": 1 - self.side}
+
+    def peer(self, step):
+        at = (self.me + step) % PLANE
+        return at, {"seq": at % 8, "win": at // 8}
+
+    def greet(self):
+        barrier = pltpu.get_barrier_semaphore()
+        pl.semaphore_signal(barrier, 1, device_id=self.partner, device_id_type=MESH)
+        for step in range(1, PLANE):
+            pl.semaphore_signal(barrier, 1, device_id=self.peer(step)[1], device_id_type=MESH)
+        pl.semaphore_wait(barrier, PLANE)
+
+
+class PlaneSum:
+    def __init__(self, copies, place, mine, slots):
+        self.place, self.mine, self.slots = place, mine, slots
+        first = copies.take(PLANE)
+        self.out, self.into = [], []
+        for step in range(1, PLANE):
+            at, device = place.peer(step)
+            self.out.append(
+                copies.remote(mine, slots.at[place.me], device, first + step, first + place.me)
+            )
+            self.into.append(copies.remote(mine, slots.at[at], device, first + step, first + at))
+
+    def start(self, rows):
+        for at, row in enumerate(rows):
+            self.mine[at : at + 1, :] = row
+        for copy in self.out:
+            copy.start()
+        self.slots[self.place.me] = self.mine[...]
+
+    def finish(self):
+        for copy in self.into:
+            copy.wait_recv()
+        total = self.slots[0]
+        for at in range(1, PLANE):
+            total = total + self.slots[at]
+        return total
+
+    def drain(self):
+        for copy in self.out:
+            copy.wait_send()
+
+
+A_MINE, B_MINE, A_OTHER, B_OTHER, MEAN, SCALE, GAIN, OFFSET, FACTOR, BETA, GAMMA = range(11)
+
+
+def first_kernel(
+    order, xin, cin, flat, w_mine, point, valid_rows, valid_ext, valid_own, vec,
+    acts, g_own, g_two, g_extra, gw, gp, rows_out,
+    xbuf, p1a, p2a, p1b, p2b, qext, ex, ec, halo_r, halo_l, hb,
+    act_m, act_o, conv, actm, gco, w_all, w_other, e_act, cat, tmp, acc1, acc2, cols,
+    msg, slots, ymsg, yin, send, recv,
+):
+    place = Place()
+    side, group, core, partner = place.side, place.group, place.core, place.partner
+    other = 1 - side
+    copies = Copies(send, recv)
+    windows, chans, bins = xbuf.shape
+    half, piece, eighth, chunk = bins // 2, bins // 4, bins // 8, bins // 4
+    base2, base3 = bins + 2 * LANES, bins + half + 4 * LANES
+    own2, own3 = bins, bins + half
+    low = lax.broadcasted_iota(jnp.int32, (ROWS, LANES), 1) < LANES // 2
+
+    def put_rows(dst, at, load, size):
+        def body(rows):
+            dst[rows, lanes_at(at, size)] = load(rows)
+
+        by_rows(chans, body)
+
+    def column(at, row):
+        cols[at] = to_column(row)
+
+    def wide(at, rows, size):
+        return spread_lanes(cols[at, rows, :], size)
+
+    loads = [copies.local(xin.at[w], xbuf.at[w]) for w in range(windows)]
+    for copy in loads:
+        copy.start()
+    place.greet()
+    share = w_other.shape[0] // PLANE
+    share_rows = lambda w, c, z, size=1: pl.ds(
+        pl.multiple_of((w * 8 + c * 4 + z) * share, share), size * share
+    )
+    mine_at = share_rows(place.win, core, group)
+    w_first = copies.remote(flat.at[mine_at], w_other.at[mine_at], partner)
+    w_first.start()
+    for copy in loads:
+        copy.wait()
+    put_rows(p1a, 0, lambda rows: xbuf[order[other], rows, :], bins)
+    x1 = [
+        copies.remote(p1a.at[:, i * chunk : (i + 1) * chunk], p2a.at[:, i * chunk : (i + 1) * chunk], partner)
+        for i in range(4)
+    ]
+    x1[0].start()
+    x1[1].start()
+    to_left = copies.remote(xbuf.at[:, :, 0:LANES], halo_r, {"seq": jnp.maximum(place.shard - 1, 0)})
+    to_right = copies.remote(xbuf.at[:, :, bins - LANES : bins], halo_l, {"seq": jnp.minimum(place.shard + 1, 7)})
+    pl.when(place.shard > 0)(to_left.start)
+    pl.when(place.shard < 7)(to_right.start)
+
+    @pl.when(place.shard == 0)
+    def _():
+        halo_l[...] = jnp.zeros_like(halo_l)
+
+    @pl.when(place.shard == 7)
+    def _():
+        halo_r[...] = jnp.zeros_like(halo_r)
+
+    acc1[...] = jnp.zeros_like(acc1)
+    acc2[...] = jnp.zeros_like(acc2)
+    for w in range(windows):
+
+        def body(rows, w=w):
+            first, second = acc1[rows, :], acc2[rows, :]
+            for at in range(0, bins, TILE):
+                x = xbuf[w, rows, at : at + TILE].astype(F32)
+                kept = x * valid_rows[w : w + 1, at : at + TILE]
+                first = first + lane_sum(kept)
+                second = second + lane_sum(kept * x)
+            acc1[rows, :] = first
+            acc2[rows, :] = second
+
+        by_rows(chans, body)
+    plane = [PlaneSum(copies, place, msg.at[i], slots.at[i]) for i in range(3)]
+    over_y = [copies.remote(ymsg.at[i], yin.at[i], partner) for i in range(3)]
+    plane[0].start([to_row(acc1[...]), to_row(acc2[...]), vec[4:5, :]])
+
+    put_rows(qext, LANES, lambda rows: xbuf[order[3], rows, :], bins)
+    w_all[:, : 3 * chans] = w_mine[...]
+    total = plane[0].finish()
+    filled = total[2:3, :]
+    ymsg[0] = jnp.concatenate([total[0:3, :], vec[0:2, :], total[0:3, :]], axis=0)
+    over_y[0].start()
+    x1[2].start()
+    x1[3].start()
+
+    def norm_of(first, second, gain, offset):
+        mean = first / filled
+        scale = lax.rsqrt(second / filled - mean * mean + EPS)
+        return mean, scale, scale * gain, offset - mean * scale * gain
+
+    mean, scale, a_mine, b_mine = norm_of(total[0:1, :], total[1:2, :], vec[0:1, :], vec[1:2, :])
+    column(A_MINE, a_mine)
+    column(B_MINE, b_mine)
+    rows_out[...] = jnp.zeros_like(rows_out)
+    rows_out[0:1, :] = mean
+    rows_out[1:2, :] = scale
+    rows_out[2:3, :] = filled
+    rows_out[6:8, :] = vec[0:2, :]
+
+    w_first.wait_recv()
+    z_first = copies.take(4)
+    w_z = []
+    for step in range(1, 4):
+        z = (group + step) % 4
+        device = {"seq": z * 2 + core}
+        out = copies.remote(
+            w_other.at[mine_at], w_other.at[mine_at], device, z_first + step, z_first + group
+        )
+        from_at = share_rows(place.win, core, z)
+        w_z.append(
+            copies.remote(w_other.at[from_at], w_other.at[from_at], device, z_first + step, z_first + z)
+        )
+        out.start()
+
+    pl.when(place.shard < 7)(to_left.wait_recv)
+    pl.when(place.shard > 0)(to_right.wait_recv)
+    put_rows(qext, 0, lambda rows: halo_l[order[3], rows, :], LANES)
+    put_rows(qext, LANES + bins, lambda rows: halo_r[order[3], rows, :], LANES)
+    ex_at, ec_at = copies.take(3), copies.take(3)
+    ex_out = [
+        copies.remote(
+            qext.at[:, k * piece : (k + 1) * piece + 2 * LANES], ex,
+            {"seq": jnp.minimum(place.shard + 2 * k, 7)}, ex_at + k - 1, ex_at,
+        )
+        for k in range(1, 4)
+    ]
+    ec_out = [
+        copies.remote(
+            qext.at[:, LANES + k * piece : LANES + (k + 1) * piece], ec,
+            {"seq": jnp.minimum(place.shard + 2 * k, 7)}, ec_at + k - 1, ec_at,
+        )
+        for k in range(1, 4)
+    ]
+
+    @pl.when(group == 0)
+    def _():
+        for copy in ex_out:
+            copy.start()
+        put_rows(ex, 0, lambda rows: qext[rows, 0 : piece + 2 * LANES], piece + 2 * LANES)
+
+    def activate(a, b, load, dst, at, size):
+        mask = valid_ext[:, lanes_at(at, size)]
+
+        def body(rows):
+            pre = load(rows).astype(F32) * wide(a, rows, size) + wide(b, rows, size)
+            dst[rows, lanes_at(at, size)] = (gelu(pre) * mask).astype(BF16)
+
+        by_rows(chans, body)
+
+    def mixed(right, left):
+        return jnp.where(low, right.astype(F32), left.astype(F32)).astype(BF16)
+
+    def first_halo(role):
+        w = order[role]
+        return lambda rows: mixed(halo_r[w, rows, :], halo_l[w, rows, :])
+
+    def second_halo(role):
+        w = order[2]
+
+        def load(rows):
+            near = xbuf[w, rows, half : half + LANES].astype(F32)
+            far = xbuf[w, rows, half - LANES : half].astype(F32)
+            right = jnp.where(role == 0, near, halo_r[w, rows, :].astype(F32))
+            left = jnp.where(role == 0, halo_l[w, rows, :].astype(F32), far)
+            return jnp.where(low, right, left).astype(BF16)
+
+        return load
+
+    def third_halo(role):
+        return lambda rows: mixed(
+            ex[rows, lanes_at(LANES + (role + 1) * eighth, LANES)], ex[rows, lanes_at(role * eighth, LANES)]
+        )
+
+    def run_segment(a, b, load, dst, at, size):
+        def body(i):
+            activate(a, b, lambda rows: load(rows, i * TILE), dst, at + i * TILE, TILE)
+
+        times(size // TILE, body)
+
+    put_rows(hb.at[0], 0, first_halo(side), LANES)
+    put_rows(hb.at[1], 0, second_halo(side), LANES)
+    activate(A_MINE, B_MINE, lambda rows: hb[0, rows, :], act_m, 0, LANES)
+    activate(A_MINE, B_MINE, lambda rows: hb[0, rows, :], act_m, LANES + bins, LANES)
+    run_segment(
+        A_MINE, B_MINE, lambda rows, at: xbuf[order[side], rows, lanes_at(at, TILE)], act_m, LANES, bins
+    )
+    put_rows(p1b, 0, first_halo(other), LANES)
+    put_rows(p1b, LANES, second_halo(other), LANES)
+    put_rows(p1b, 2 * LANES, lambda rows: xbuf[order[2], rows, lanes_at(other * half, half)], half)
+    cuts2 = (0, 2 * LANES + half // 2, 2 * LANES + half, 3 * LANES + half + eighth)
+    x2 = [copies.remote(p1b.at[:, lo:hi], p2b.at[:, lo:hi], partner) for lo, hi in zip(cuts2, cuts2[1:])]
+    x2[0].start()
+    for copy in w_z:
+        copy.wait_recv()
+    block = share_rows(place.win, core, 0, 4)
+    block_in = share_rows(1 - place.win, core, 0, 4)
+    across = {"win": 1 - place.win}
+    w_x_at = copies.take()
+    w_x = copies.remote(w_other.at[block], w_other.at[block], across, w_x_at, w_x_at)
+    w_x_in = copies.remote(w_other.at[block_in], w_other.at[block_in], across, w_x_at, w_x_at)
+    w_x.start()
+    activate(A_MINE, B_MINE, lambda rows: hb[1, rows, :], act_m, base2, LANES)
+    activate(A_MINE, B_MINE, lambda rows: hb[1, rows, :], act_m, base2 + LANES + half, LANES)
+    run_segment(
+        A_MINE, B_MINE, lambda rows, at: xbuf[order[2], rows, lanes_at(side * half + at, TILE)],
+        act_m, base2 + LANES, half,
+    )
+    pl.when(place.shard > 0)(to_left.wait_send)
+    pl.when(place.shard < 7)(to_right.wait_send)
+    cot_loads = [copies.local(cin.at[w], xbuf.at[w]) for w in range(windows)]
+    for copy in cot_loads:
+        copy.start()
+    w_x_in.wait_recv()
+    sibling = {"seq": group * 2 + 1 - core}
+    w_c_at = [copies.take() for _ in range(2)]
+    w_c, w_c_in = [], []
+    for w in range(2):
+        rows = share_rows(w, core, 0, 4)
+        rows_in = share_rows(w, 1 - core, 0, 4)
+        w_c.append(copies.remote(w_other.at[rows], w_other.at[rows], sibling, w_c_at[w], w_c_at[w]))
+        w_c_in.append(
+            copies.remote(w_other.at[rows_in], w_other.at[rows_in], sibling, w_c_at[w], w_c_at[w])
+        )
+        w_c[w].start()
+
+    over_y[0].wait_recv()
+    _, _, a_other, b_other = norm_of(*(yin[0, i : i + 1, :] for i in (0, 1, 3, 4)))
+    column(A_OTHER, a_other)
+    column(B_OTHER, b_other)
+    for copy in w_c_in:
+        copy.wait_recv()
+    for tap in range(3):
+        w_all[:, (3 + tap) * chans : (4 + tap) * chans] = jnp.transpose(
+            w_other[tap * chans : (tap + 1) * chans, :]
+        )
+    for i in range(4):
+        x1[i].wait_recv()
+        run_segment(
+            A_OTHER, B_OTHER, lambda rows, at, i=i: p2a[rows, lanes_at(i * chunk + at, TILE)],
+            act_o, LANES + i * chunk, chunk,
+        )
+        if i == 2:
+            for copy in x1:
+                copy.wait_send()
+            x2[1].start()
+    pl.when(group > 0)(lambda: ex_out[0].wait_recv())
+    put_rows(p1b, cuts2[2], third_halo(other), LANES)
+    put_rows(
+        p1b, cuts2[2] + LANES, lambda rows: ex[rows, lanes_at(LANES + other * eighth, eighth)], eighth
+    )
+    x2[2].start()
+    put_rows(hb.at[2], 0, third_halo(side), LANES)
+    activate(A_MINE, B_MINE, lambda rows: hb[2, rows, :], act_m, base3, LANES)
+    activate(A_MINE, B_MINE, lambda rows: hb[2, rows, :], act_m, base3 + LANES + eighth, LANES)
+    run_segment(
+        A_MINE, B_MINE, lambda rows, at: ex[rows, lanes_at(LANES + side * eighth + at, TILE)],
+        act_m, base3 + LANES, eighth,
+    )
+    for copy in cot_loads:
+        copy.wait()
+    put_rows(p2a, 0, lambda rows: xbuf[order[other], rows, :], bins)
+
+    @pl.when(group == 0)
+    def _():
+        for copy in ex_out:
+            copy.wait_send()
+
+    put_rows(qext, LANES, lambda rows: xbuf[order[3], rows, :], bins)
+
+    @pl.when(group == 0)
+    def _():
+        for copy in ec_out:
+            copy.start()
+        put_rows(ec, 0, lambda rows: qext[rows, LANES : LANES + piece], piece)
+
+    def fill_taps(start):
+        for at_half, ref in enumerate((act_m, act_o)):
+            cells = ref[:, lanes_at(start, TILE + 2 * LANES)]
+            for tap in range(3):
+                at = LANES + (tap - 1) * DILATION_BINS
+                row = (at_half * 3 + tap) * chans
+                cat[row : row + chans, :] = cells[:, at : at + TILE]
+
+    def conv_tiles(start, own, count):
+        def body(i):
+            fill_taps(start + i * TILE)
+            out = dot(w_all[...], cat[...])
+            conv[:, lanes_at(own + i * TILE, TILE)] = out
+            kept = out * valid_own[:, lanes_at(own + i * TILE, TILE)]
+            acc1[...] += lane_sum(kept)
+            acc2[...] += lane_sum(kept * out)
+
+        times(count, body)
+
+    acc1[...] = jnp.zeros_like(acc1)
+    acc2[...] = jnp.zeros_like(acc2)
+    x2[0].wait_recv()
+    other_halo = lambda at: lambda rows: p2b[rows, at : at + LANES]
+    activate(A_OTHER, B_OTHER, other_halo(0), act_o, 0, LANES)
+    activate(A_OTHER, B_OTHER, other_halo(0), act_o, LANES + bins, LANES)
+    activate(A_OTHER, B_OTHER, other_halo(LANES), act_o, base2, LANES)
+    activate(A_OTHER, B_OTHER, other_halo(LANES), act_o, base2 + LANES + half, LANES)
+    other_second = lambda rows, at: p2b[rows, lanes_at(2 * LANES + at, TILE)]
+    run_segment(A_OTHER, B_OTHER, other_second, act_o, base2 + LANES, half // 2)
+    conv_tiles(0, 0, bins // TILE)
+    x2[1].wait_recv()
+    c1 = [
+        copies.remote(p2a.at[:, i * chunk : (i + 1) * chunk], p1a.at[:, i * chunk : (i + 1) * chunk], partner)
+        for i in range(4)
+    ]
+    c1[0].start()
+    c1[1].start()
+    run_segment(
+        A_OTHER, B_OTHER, lambda rows, at: other_second(rows, half // 2 + at),
+        act_o, base2 + LANES + half // 2, half // 2,
+    )
+    conv_tiles(base2, own2, half // TILE)
+    x2[2].wait_recv()
+    activate(A_OTHER, B_OTHER, other_halo(cuts2[2]), act_o, base3, LANES)
+    activate(A_OTHER, B_OTHER, other_halo(cuts2[2]), act_o, base3 + LANES + eighth, LANES)
+    run_segment(
+        A_OTHER, B_OTHER, lambda rows, at: p2b[rows, lanes_at(cuts2[2] + LANES + at, TILE)],
+        act_o, base3 + LANES, eighth,
+    )
+    conv_tiles(base3, own3, eighth // TILE)
+    plane[1].start([to_row(acc1[...]), to_row(acc2[...])])
+    for copy in x2:
+        copy.wait_send()
+    c1[2].start()
+
+    acc1[...] = jnp.zeros_like(acc1)
+    for w in range(windows):
+
+        def body(rows, w=w):
+            acc1[rows, :] += lane_sum(xbuf[w, rows, :].astype(F32))
+
+        by_rows(chans, body)
+    bias_row = to_row(acc1[...])
+    total = plane[1].finish()
+    ymsg[1] = total
+    over_y[1].start()
+    c1[3].start()
+    pl.when(group > 0)(lambda: ec_out[0].wait_recv())
+    put_rows(p2b, 0, lambda rows: xbuf[order[2], rows, lanes_at(other * half, half)], half)
+    put_rows(p2b, half, lambda rows: ec[rows, lanes_at(other * eighth, eighth)], eighth)
+    cuts = (0, half // 2, half, half + eighth)
+    c2 = [copies.remote(p2b.at[:, lo:hi], p1b.at[:, lo:hi], partner) for lo, hi in zip(cuts, cuts[1:])]
+    c1[2].wait_recv()
+    c2[0].start()
+
+    over_y[1].wait_recv()
+    total = ymsg[1] + yin[1]
+    gain_mid, offset_mid = vec[2:3, :], vec[3:4, :]
+    mean = total[0:1, :] / filled
+    scale = lax.rsqrt(total[1:2, :] / filled - mean * mean + EPS)
+    for at, row in ((MEAN, mean), (SCALE, scale), (GAIN, gain_mid), (OFFSET, offset_mid), (FACTOR, gain_mid * scale)):
+        column(at, row)
+
+    def act_tile(i):
+        at = lanes_at(i * TILE, TILE)
+        mask = valid_own[:, at]
+
+        def body(rows):
+            norm = (conv[rows, at] - wide(MEAN, rows, TILE)) * wide(SCALE, rows, TILE)
+            pre = norm * wide(GAIN, rows, TILE) + wide(OFFSET, rows, TILE)
+            actm[rows, at] = (gelu(pre) * mask).astype(BF16)
+
+        by_rows(chans, body)
+
+    times(conv.shape[1] // TILE, act_tile)
+    keeps = [
+        copies.local(actm.at[:, 0:bins], acts.at[side]),
+        copies.local(actm.at[:, own2:own3], acts.at[2, :, lanes_at(side * half, half)]),
+    ]
+    for copy in keeps:
+        copy.start()
+
+    acc1[...] = jnp.zeros_like(acc1)
+    acc2[...] = jnp.zeros_like(acc2)
+    gp[...] = jnp.zeros_like(gp)
+
+    def back_product(mine, theirs):
+        cat[0:chans, :] = mine
+        cat[chans : 2 * chans, :] = theirs
+        tmp[...] = dot(point[...], cat[0:chans, :]) + dot(w_other[3 * chans :, :], cat[chans : 2 * chans, :])
+
+    def grad_rows(rows, at, mask):
+        norm = (conv[rows, at] - wide(MEAN, rows, TILE)) * wide(SCALE, rows, TILE)
+        pre = norm * wide(GAIN, rows, TILE) + wide(OFFSET, rows, TILE)
+        return norm, mask * gelu_slope(pre) * tmp[rows, :]
+
+    def sum_tile(mine, theirs, own):
+        back_product(mine, theirs)
+        at = lanes_at(own, TILE)
+        mask = valid_own[:, at]
+
+        def body(rows):
+            norm, part = grad_rows(rows, at, mask)
+            acc1[rows, :] += lane_sum(part)
+            acc2[rows, :] += lane_sum(part * norm)
+
+        by_rows(chans, body)
+        gp[...] += dot_t(actm[:, at], cat[0 : 2 * chans, :])
+
+    def grad_tile(mine, theirs, own):
+        back_product(mine, theirs)
+        at = lanes_at(own, TILE)
+        mask = valid_own[:, at]
+
+        def body(rows):
+            norm, part = grad_rows(rows, at, mask)
+            kept = mask * (wide(BETA, rows, TILE) + norm * wide(GAMMA, rows, TILE))
+            gco[rows, at] = (wide(FACTOR, rows, TILE) * (part - kept)).astype(BF16)
+
+        by_rows(chans, body)
+
+    def over_first(run, lo, hi):
+        def body(i):
+            at = lanes_at(lo + i * TILE, TILE)
+            run(xbuf[order[side], :, at], p1a[:, at], lo + i * TILE)
+
+        times((hi - lo) // TILE, body)
+
+    def over_second(run, lo, hi):
+        def body(i):
+            at = lo + i * TILE
+            run(
+                xbuf[order[2], :, lanes_at(side * half + at, TILE)], p1b[:, lanes_at(at, TILE)], own2 + at
+            )
+
+        times((hi - lo) // TILE, body)
+
+    def over_third(run):
+        run(ec[:, lanes_at(side * eighth, TILE)], p1b[:, half : half + TILE], own3)
+
+    t3_extra = copies.remote(actm.at[:, own3:], e_act, partner)
+    t3 = [
+        copies.remote(
+            actm.at[:, own2 + i * TILE : own2 + (i + 1) * TILE],
+            acts.at[2, :, lanes_at(side * half + i * TILE, TILE)],
+            partner,
+        )
+        for i in range(half // TILE)
+    ]
+    for i in range(4):
+        if i != 2:
+            c1[i].wait_recv()
+        if i == 3:
+            c2[1].start()
+            c2[2].start()
+        over_first(sum_tile, i * chunk, (i + 1) * chunk)
+    c2[0].wait_recv()
+    over_second(sum_tile, 0, half // 2)
+    c2[1].wait_recv()
+    t3_extra.start()
+    t3[0].start()
+    over_second(sum_tile, half // 2, half)
+    c2[2].wait_recv()
+    over_third(sum_tile)
+    plane[2].start([to_row(acc1[...]), to_row(acc2[...]), bias_row])
+    total = plane[2].finish()
+    ymsg[2] = total
+    over_y[2].start()
+    for copy in t3[1:]:
+        copy.start()
+    over_y[2].wait_recv()
+    beta = ymsg[2, 0:1, :] + yin[2, 0:1, :]
+    gamma = ymsg[2, 1:2, :] + yin[2, 1:2, :]
+    rows_out[3:4, :] = beta
+    rows_out[4:5, :] = gamma
+    rows_out[5:6, :] = ymsg[2, 2:3, :]
+    column(BETA, beta / filled)
+    column(GAMMA, gamma / filled)
+
+    over_third(grad_tile)
+    t4_extra = copies.remote(gco.at[:, own3:], g_extra, partner)
+    t4_extra.start()
+    over_second(grad_tile, 0, half // 2)
+    t4 = copies.remote(gco.at[:, own2 : own2 + half // 2], g_two, partner)
+    t4.start()
+    over_second(grad_tile, half // 2, half)
+    over_first(grad_tile, 0, bins)
+    g_keep = copies.local(gco, g_own)
+    g_keep.start()
+
+    back_to = {"seq": core}
+    e_at = copies.take(8)
+    t3_extra.wait_recv()
+    e_home = [
+        copies.remote(
+            src, acts.at[3, :, lanes_at(group * piece + role * eighth, eighth)], back_to,
+            e_at + which, e_at + 2 * group + which,
+        )
+        for which, (src, role) in enumerate(((actm.at[:, own3:], side), (e_act, other)))
+    ]
+    e_mine = [
+        copies.local(src, acts.at[3, :, lanes_at(role * eighth, eighth)])
+        for src, role in ((actm.at[:, own3:], side), (e_act, other))
+    ]
+
+    @pl.when(group > 0)
+    def _():
+        for copy in e_home:
+            copy.start()
+
+    @pl.when(group == 0)
+    def _():
+        for copy in e_mine:
+            copy.start()
+
+    weight_sum = conv.at[:, 0 : 6 * chans]
+    weight_sum[...] = jnp.zeros_like(weight_sum)
+
+    def weight_tiles(start, own, count):
+        def body(i):
+            fill_taps(start + i * TILE)
+            weight_sum[...] += dot_t(gco[:, lanes_at(own + i * TILE, TILE)], cat[...])
+
+        times(count, body)
+
+    weight_tiles(0, 0, bins // TILE)
+    weight_tiles(base2, own2, half // TILE)
+    weight_tiles(base3, own3, eighth // TILE)
+
+    gw_keep = copies.local(weight_sum, gw)
+    gw_keep.start()
+
+    @pl.when(group > 0)
+    def _():
+        for copy in e_home:
+            copy.wait_send()
+
+    @pl.when(group == 0)
+    def _():
+        for copy in e_mine:
+            copy.wait()
+        for copy in ec_out:
+            copy.wait_send()
+        for z in range(1, 4):
+            for which, role in enumerate((side, other)):
+                at = acts.at[3, :, lanes_at(z * piece + role * eighth, eighth)]
+                copies.remote(at, at, back_to, e_at, e_at + 2 * z + which).wait_recv()
+
+    for copy in keeps + [g_keep, gw_keep]:
+        copy.wait()
+    for copy in plane:
+        copy.drain()
+    for copy in [w_first, w_x, *w_c, *w_z, *over_y, *c1, *c2, t3_extra, *t3, t4_extra, t4]:
+        copy.wait_send()
+    for copy in [*t3, t4_extra, t4]:
+        copy.wait_recv()
+
+
+def second_kernel(
+    order, xin, acts_in, g_own, g_two, g_extra, gw, gp, weight, valid, rows_in,
+    acts, grads, rows_out, conv_grad, point_grad,
+    gs, xbuf, halo_r, halo_l, cat, tmp, acc1, acc2, cols, msg, slots,
+    parts, parts_core, parts_win, parts_z, parts_side, summed, send, recv,
+):
+    del acts_in
+    place = Place()
+    side, group, core, partner = place.side, place.group, place.core, place.partner
+    other = 1 - side
+    copies = Copies(send, recv)
+    windows, chans, bins = xbuf.shape
+    half, piece, eighth, chunk = bins // 2, bins // 4, bins // 8, bins // 4
+    own2, own3 = bins, bins + half
+
+    own_loads = [
+        copies.local(g_own.at[:, 0:bins], gs.at[side, :, LANES : LANES + bins]),
+        copies.local(g_own.at[:, own2:own3], gs.at[2, :, lanes_at(LANES + side * half, half)]),
+        copies.local(g_two, gs.at[2, :, lanes_at(LANES + other * half, half // 2)]),
+    ]
+    extra = ((g_own.at[:, own3:], side), (g_extra, other))
+    extra_loads = [
+        copies.local(src, gs.at[3, :, lanes_at(LANES + role * eighth, eighth)]) for src, role in extra
+    ]
+    loads = [copies.local(xin.at[w], xbuf.at[w]) for w in range(windows)]
+    depth = conv_grad.shape[0] * chans
+    part_loads = [copies.local(gw.at[:, i * depth : (i + 1) * depth], parts.at[i, :, :depth]) for i in (0, 1)]
+    part_loads += [copies.local(gp.at[:, i * chans : (i + 1) * chans], parts.at[i, :, depth:]) for i in (0, 1)]
+    for copy in own_loads + loads + part_loads:
+        copy.start()
+
+    @pl.when(group == 0)
+    def _():
+        for copy in extra_loads:
+            copy.start()
+
+    place.greet()
+    t4 = copies.remote(
+        g_own.at[:, own2 + half // 2 : own3],
+        gs.at[2, :, lanes_at(LANES + side * half + half // 2, half // 2)],
+        partner,
+    )
+    t4_first = [
+        copies.remote(
+            g_own.at[:, i * chunk : (i + 1) * chunk],
+            gs.at[side, :, LANES + i * chunk : LANES + (i + 1) * chunk],
+            partner,
+        )
+        for i in range(4)
+    ]
+    t3_first = []
+    for i in range(4):
+        at = acts.at[side, :, i * chunk : (i + 1) * chunk]
+        t3_first.append(copies.remote(at, at, partner))
+    t4.start()
+    for copy in t4_first:
+        copy.start()
+    t3_first[0].start()
+
+    tail = parts_side.shape[0]
+    core_rows = lambda c: pl.ds(pl.multiple_of(8 * tail * c, tail), 8 * tail)
+    win_rows = lambda w: pl.ds(pl.multiple_of(8 * tail * core + 4 * tail * w, tail), 4 * tail)
+    z_rows = lambda z: pl.ds(
+        pl.multiple_of(8 * tail * core + 4 * tail * place.win + tail * z, tail), tail
+    )
+    sibling, across = {"seq": group * 2 + 1 - core}, {"win": 1 - place.win}
+    s_core = copies.remote(parts.at[:, core_rows(1 - core), :], parts_core, sibling)
+    s_win = copies.remote(parts.at[:, win_rows(1 - place.win), :], parts_win, across)
+    s_z_at = copies.take(4)
+    s_z, s_z_in = [], []
+    g_z_at = copies.take(4)
+    g_z, g_z_in = [], []
+    for step in range(1, 4):
+        z = (group + step) % 4
+        device = {"seq": z * 2 + core}
+        s_z.append(
+            copies.remote(parts.at[:, z_rows(z), :], parts_z.at[group], device, s_z_at + step, s_z_at + group)
+        )
+        s_z_in.append(
+            copies.remote(parts.at[:, z_rows(z), :], parts_z.at[z], device, s_z_at + step, s_z_at + z)
+        )
+        g_z.append(
+            copies.remote(
+                summed.at[z_rows(group), :], summed.at[z_rows(group), :], device, g_z_at + step, g_z_at + group
+            )
+        )
+        g_z_in.append(
+            copies.remote(summed.at[z_rows(z), :], summed.at[z_rows(z), :], device, g_z_at + step, g_z_at + z)
+        )
+    s_side = copies.remote(parts.at[1, z_rows(group), :], parts_side, partner)
+    g_win_at, g_core_at = copies.take(), copies.take()
+    both = lambda at, rows, rows_in, device: tuple(
+        copies.remote(summed.at[r, :], summed.at[r, :], device, at, at) for r in (rows, rows_in)
+    )
+    g_win, g_win_in = both(g_win_at, win_rows(place.win), win_rows(1 - place.win), across)
+    g_core, g_core_in = both(g_core_at, core_rows(core), core_rows(1 - core), sibling)
+    for copy in part_loads:
+        copy.wait()
+    s_core.start()
+
+    class Halo:
+        def __init__(self, slot, last):
+            self.slot, self.last = slot, last
+            self.left = copies.remote(
+                gs.at[slot, :, LANES : 2 * LANES], halo_r.at[slot], {"seq": jnp.maximum(place.shard - 1, 0)}
+            )
+            self.right = copies.remote(
+                gs.at[slot, :, bins : bins + LANES], halo_l.at[slot], {"seq": jnp.minimum(place.shard + 1, 7)}
+            )
+
+        def start(self):
+            pl.when((place.shard > 0) & (place.shard <= self.last))(self.left.start)
+            pl.when(place.shard < self.last)(self.right.start)
+
+        def finish(self):
+            @pl.when(place.shard < self.last)
+            def _():
+                self.left.wait_recv()
+                gs[self.slot, :, LANES + bins :] = halo_r[self.slot]
+
+            @pl.when(place.shard >= self.last)
+            def _():
+                gs[self.slot, :, LANES + bins :] = jnp.zeros((chans, LANES), BF16)
+
+            @pl.when(place.shard > 0)
+            def _():
+                self.right.wait_recv()
+                gs[self.slot, :, 0:LANES] = halo_l[self.slot]
+
+            @pl.when(place.shard == 0)
+            def _():
+                gs[self.slot, :, 0:LANES] = jnp.zeros((chans, LANES), BF16)
+
+            pl.when((place.shard > 0) & (place.shard <= self.last))(self.left.wait_send)
+            pl.when(place.shard < self.last)(self.right.wait_send)
+
+    halos = {name: Halo(slot, last) for name, slot, last in (("own", side, 7), ("third", 2, 7), ("other", other, 7), ("quarter", 3, 1))}
+    own_loads[0].wait()
+    halos["own"].start()
+    e_at = copies.take(8)
+    back_to = {"seq": core}
+    e_home = [
+        copies.remote(
+            src, gs.at[3, :, lanes_at(LANES + group * piece + role * eighth, eighth)], back_to,
+            e_at + which, e_at + 2 * group + which,
+        )
+        for which, (src, role) in enumerate(extra)
+    ]
+
+    @pl.when(group > 0)
+    def _():
+        for copy in e_home:
+            copy.start()
+
+    names = {"mean": 0, "scale": 1, "gain": 2, "offset": 3}
+    for at, row in enumerate((0, 1, 6, 7)):
+        cols[at] = to_column(rows_in[row : row + 1, :])
+    wide = lambda name, rows: spread_lanes(cols[names[name], rows, :], TILE)
+    acc1[...] = jnp.zeros_like(acc1)
+    acc2[...] = jnp.zeros_like(acc2)
+
+    def through(slot):
+        def tile(i):
+            cells = gs[slot, :, lanes_at(i * TILE, TILE + 2 * LANES)]
+            for tap in range(3):
+                at = LANES - (tap - 1) * DILATION_BINS
+                cat[tap * chans : (tap + 1) * chans, :] = cells[:, at : at + TILE]
+            tmp[...] = dot(weight[...], cat[...])
+            at = lanes_at(i * TILE, TILE)
+            mask = valid[pl.ds(slot, 1), at]
+            window = order[slot]
+
+            def body(rows):
+                norm = (xbuf[window, rows, at].astype(F32) - wide("mean", rows)) * wide("scale", rows)
+                part = mask * gelu_slope(norm * wide("gain", rows) + wide("offset", rows)) * tmp[rows, :]
+                acc1[rows, :] += lane_sum(part)
+                acc2[rows, :] += lane_sum(part * norm)
+                gs[slot, rows, at] = part.astype(BF16)
+
+            by_rows(chans, body)
+
+        times(bins // TILE, tile)
+
+    keeps = []
+
+    def keep(slot):
+        copy = copies.local(gs.at[slot, :, 0:bins], grads.at[slot])
+        copy.start()
+        keeps.append(copy)
+
+    for copy in loads:
+        copy.wait()
+    halos["own"].finish()
+    through(side)
+    keep(side)
+    s_core.wait_recv()
+    parts[:, core_rows(core), :] += parts_core[...]
+    s_win.start()
+    own_loads[1].wait()
+    own_loads[2].wait()
+    t4.wait_recv()
+    halos["third"].start()
+    quarter_keep = copies.local(gs.at[3, :, 0:bins], grads.at[3])
+
+    @pl.when(group == 0)
+    def _():
+        for copy in extra_loads:
+            copy.wait()
+        for z in range(1, 4):
+            for which, role in enumerate((side, other)):
+                at = gs.at[3, :, lanes_at(LANES + z * piece + role * eighth, eighth)]
+                copies.remote(at, at, back_to, e_at, e_at + 2 * z + which).wait_recv()
+        halos["quarter"].start()
+
+    halos["third"].finish()
+    through(2)
+    keep(2)
+    s_win.wait_recv()
+    parts[:, win_rows(place.win), :] += parts_win[...]
+    for copy in s_z:
+        copy.start()
+
+    @pl.when(group == 0)
+    def _():
+        halos["quarter"].finish()
+        through(3)
+        quarter_keep.start()
+
+    for copy in s_z_in:
+        copy.wait_recv()
+    parts_z[group] = parts[:, z_rows(group), :]
+    total = parts_z[0]
+    for z in range(1, 4):
+        total = total + parts_z[z]
+    parts[:, z_rows(group), :] = total
+    s_side.start()
+    for copy in t3_first[1:]:
+        copy.start()
+    for copy in t4_first:
+        copy.wait_recv()
+    halos["other"].start()
+    halos["other"].finish()
+    s_side.wait_recv()
+    summed[z_rows(group), :] = parts[0, z_rows(group), :] + parts_side[...]
+    for copy in g_z:
+        copy.start()
+    through(other)
+    keep(other)
+    plane = PlaneSum(copies, place, msg, slots)
+    plane.start([to_row(acc1[...]), to_row(acc2[...])])
+    for copy in g_z_in:
+        copy.wait_recv()
+    g_win.start()
+    rows_out[...] = plane.finish()
+    g_win_in.wait_recv()
+    g_core.start()
+    plane.drain()
+    g_core_in.wait_recv()
+    for tap in range(conv_grad.shape[0]):
+        conv_grad[tap] = jnp.transpose(summed[:, tap * chans : (tap + 1) * chans])
+    point_grad[...] = summed[:, depth:]
+    for copy in [s_core, s_win, s_side, *s_z, *g_z, g_win, g_core]:
+        copy.wait_send()
+    for copy in keeps:
+        copy.wait()
+
+    @pl.when(group == 0)
+    def _():
+        quarter_keep.wait()
+
+    @pl.when(group > 0)
+    def _():
+        for copy in e_home:
+            copy.wait_send()
+
+    for copy in [t4, *t4_first, *t3_first]:
+        copy.wait_send()
+    for copy in t3_first:
+        copy.wait_recv()
+
+
+def last_kernel(slot, x, c, act, grad, valid, weight, rows_one, rows_two, bias, out, grad_out, cols, tmp):
+    del slot
+
+    @pl.when((pl.program_id(0) == 0) & (pl.program_id(1) == 0))
+    def _():
+        mean, scale, filled, gain = (rows_one[i : i + 1, :] for i in (0, 1, 2, 6))
+        for at, row in enumerate(
+            (mean, scale, gain * scale, rows_two[0:1, :] / filled, rows_two[1:2, :] / filled, bias[...])
+        ):
+            cols[at] = to_column(row)
+
+    mask = valid[0] > 0.0
+    size = x.shape[2]
+    cells = jnp.where(mask, act[0].astype(F32), 0.0).astype(BF16)
+    tmp[...] = dot(weight[...], cells)
+    wide = lambda at, rows: spread_lanes(cols[at, rows, :], size)
+
+    def body(rows):
+        xs = x[0, rows, :].astype(F32)
+        out[0, rows, :] = (xs + tmp[rows, :] + wide(5, rows)).astype(BF16)
+        norm = (xs - wide(0, rows)) * wide(1, rows)
+        back = wide(2, rows) * (grad[0, rows, :].astype(F32) - (wide(3, rows) + norm * wide(4, rows)))
+        grad_out[0, rows, :] = (c[0, rows, :].astype(F32) + jnp.where(mask, back, 0.0)).astype(BF16)
+
+    by_rows(x.shape[1], body)
+
+
+def local_pair(
+    inputs,
+    lengths,
+    gain_in,
+    offset_in,
+    conv_weight,
+    gain_mid,
+    offset_mid,
+    point_weight,
+    point_bias,
+    cotangent,
+):
+    windows, chans, bins = inputs.shape
+    taps, _, bottle = conv_weight.shape
+    side, shard, _ = (lax.axis_index(name) for name in ("ch", "seq", "win"))
+    group = shard // 2
+    piece, half, eighth = bins // 4, bins // 2, bins // 8
+    widened, packed = bins + half + eighth + 6 * LANES, bins + half + eighth
+
+    ids = jnp.arange(windows, dtype=jnp.int32)
+    ahead = (lengths[None, :] > lengths[:, None]) | (
+        (lengths[None, :] == lengths[:, None]) & (ids[None, :] < ids[:, None])
+    )
+    rank = jnp.sum(ahead.astype(jnp.int32), axis=1)
+    chosen = rank[None, :] == ids[:, None]
+    order = jnp.sum(jnp.where(chosen, ids[None, :], 0), axis=1)
+    ranked = jnp.sum(jnp.where(chosen, lengths[None, :], 0), axis=1)
+
+    places = shard * bins + jnp.arange(bins, dtype=jnp.int32)
+    valid_rows = (places[None, :] < lengths[:, None]).astype(F32)
+    valid_slots = (places[None, :] < ranked[:, None]).astype(F32)
+    starts = (
+        shard * bins,
+        shard * bins + side * half,
+        (shard % 2) * bins + group * piece + side * eighth,
+    )
+    limits = (jnp.where(side == 0, ranked[0], ranked[1]), ranked[2], ranked[3])
+    spots = jnp.concatenate(
+        [
+            at - LANES + jnp.arange(size + 2 * LANES, dtype=jnp.int32)
+            for at, size in zip(starts, (bins, half, eighth), strict=True)
+        ]
+    )
+    limit = jnp.concatenate(
+        [
+            jnp.full((size + 2 * LANES,), at, jnp.int32)
+            for at, size in zip(limits, (bins, half, eighth), strict=True)
+        ]
+    )
+    valid_ext = ((spots >= 0) & (spots < limit)).astype(F32)[None, :]
+    valid_own = jnp.concatenate(
+        [
+            valid_ext[:, at : at + size]
+            for at, size in (
+                (LANES, bins),
+                (bins + 3 * LANES, half),
+                (bins + half + 5 * LANES, eighth),
+            )
+        ],
+        axis=1,
+    )
+    kept = jnp.sum(jnp.clip(lengths - shard * bins, 0, bins)).astype(F32)
+    zero = jnp.zeros((chans,), F32)
+    vec = jnp.stack(
+        [gain_in, offset_in, gain_mid, offset_mid, jnp.full((chans,), kept), zero, zero, zero]
+    )
+    turn = lambda w: jnp.transpose(w, (2, 0, 1)).reshape(bottle, taps * chans)
+    flat = jnp.concatenate([conv_weight.reshape(taps * chans, bottle), point_weight], axis=0)
+
+    vmem = pl.BlockSpec(memory_space=pltpu.VMEM)
+    hbm = pl.BlockSpec(memory_space=pl.ANY)
+    smem = pl.BlockSpec(memory_space=pltpu.SMEM)
+    shape = jax.ShapeDtypeStruct
+    acts, g_own, g_two, g_extra, gw, gp, rows_one = pl.pallas_call(
+        first_kernel,
+        in_specs=[smem, hbm, hbm, hbm, vmem, vmem, vmem, vmem, vmem, vmem],
+        out_specs=[hbm, hbm, hbm, hbm, hbm, vmem, vmem],
+        out_shape=[
+            shape((windows, bottle, bins), BF16),
+            shape((bottle, packed), BF16),
+            shape((bottle, half // 2), BF16),
+            shape((bottle, eighth), BF16),
+            shape((bottle, 2 * taps * chans), F32),
+            shape((bottle, 2 * chans), F32),
+            shape((8, chans), F32),
+        ],
+        scratch_shapes=[
+            pltpu.VMEM((windows, chans, bins), BF16),
+            pltpu.VMEM((chans, bins), BF16),
+            pltpu.VMEM((chans, bins), BF16),
+            pltpu.VMEM((chans, half + eighth + 3 * LANES), BF16),
+            pltpu.VMEM((chans, half + eighth + 3 * LANES), BF16),
+            pltpu.VMEM((chans, bins + 2 * LANES), BF16),
+            pltpu.VMEM((chans, piece + 2 * LANES), BF16),
+            pltpu.VMEM((chans, piece), BF16),
+            pltpu.VMEM((windows, chans, LANES), BF16),
+            pltpu.VMEM((windows, chans, LANES), BF16),
+            pltpu.VMEM((3, chans, LANES), BF16),
+            pltpu.VMEM((chans, widened), BF16),
+            pltpu.VMEM((chans, widened), BF16),
+            pltpu.VMEM((bottle, packed), F32),
+            pltpu.VMEM((bottle, packed), BF16),
+            pltpu.VMEM((bottle, packed), BF16),
+            pltpu.VMEM((bottle, 2 * taps * chans), BF16),
+            pltpu.VMEM(((taps + 1) * chans, bottle), BF16),
+            pltpu.VMEM((bottle, eighth), BF16),
+            pltpu.VMEM((2 * taps * chans, TILE), BF16),
+            pltpu.VMEM((bottle, TILE), F32),
+            pltpu.VMEM((chans, LANES), F32),
+            pltpu.VMEM((chans, LANES), F32),
+            pltpu.VMEM((11, chans, LANES), F32),
+            pltpu.VMEM((3, 8, chans), F32),
+            pltpu.VMEM((3, PLANE, 8, chans), F32),
+            pltpu.VMEM((3, 8, chans), F32),
+            pltpu.VMEM((3, 8, chans), F32),
+            pltpu.SemaphoreType.DMA((128,)),
+            pltpu.SemaphoreType.DMA((128,)),
+        ],
+        compiler_params=pltpu.CompilerParams(
+            collective_id=0, has_side_effects=True, vmem_limit_bytes=VMEM_BYTES
+        ),
+        cost_estimate=pl.CostEstimate(flops=60 * 10**9, bytes_accessed=10**8, transcendentals=0),
+    )(
+        order, inputs, cotangent, flat, turn(conv_weight), point_weight,
+        valid_rows, valid_ext, valid_own, vec,
+    )
+
+    weight_back = jnp.transpose(conv_weight, (1, 0, 2)).reshape(chans, taps * bottle)
+    share = bottle // PLANE
+    acts, grads, rows_two, conv_grad, point_grad = pl.pallas_call(
+        second_kernel,
+        in_specs=[smem, hbm, hbm, hbm, hbm, hbm, hbm, hbm, vmem, vmem, vmem],
+        out_specs=[hbm, hbm, vmem, vmem, vmem],
+        out_shape=[
+            shape((windows, bottle, bins), BF16),
+            shape((windows, chans, bins), BF16),
+            shape((8, chans), F32),
+            shape((taps, chans, bottle), F32),
+            shape((bottle, chans), F32),
+        ],
+        input_output_aliases={2: 0},
+        scratch_shapes=[
+            pltpu.VMEM((windows, bottle, bins + 2 * LANES), BF16),
+            pltpu.VMEM((windows, chans, bins), BF16),
+            pltpu.VMEM((windows, bottle, LANES), BF16),
+            pltpu.VMEM((windows, bottle, LANES), BF16),
+            pltpu.VMEM((taps * bottle, TILE), BF16),
+            pltpu.VMEM((chans, TILE), F32),
+            pltpu.VMEM((chans, LANES), F32),
+            pltpu.VMEM((chans, LANES), F32),
+            pltpu.VMEM((4, chans, LANES), F32),
+            pltpu.VMEM((8, chans), F32),
+            pltpu.VMEM((PLANE, 8, chans), F32),
+            pltpu.VMEM((2, bottle, (taps + 1) * chans), F32),
+            pltpu.VMEM((2, bottle // 2, (taps + 1) * chans), F32),
+            pltpu.VMEM((2, bottle // 4, (taps + 1) * chans), F32),
+            pltpu.VMEM((4, 2, share, (taps + 1) * chans), F32),
+            pltpu.VMEM((share, (taps + 1) * chans), F32),
+            pltpu.VMEM((bottle, (taps + 1) * chans), F32),
+            pltpu.SemaphoreType.DMA((128,)),
+            pltpu.SemaphoreType.DMA((128,)),
+        ],
+        compiler_params=pltpu.CompilerParams(
+            collective_id=1, has_side_effects=True, vmem_limit_bytes=52 * 1000 * 1000
+        ),
+        cost_estimate=pl.CostEstimate(flops=60 * 10**9, bytes_accessed=10**8, transcendentals=0),
+    )(order, inputs, acts, g_own, g_two, g_extra, gw, gp, weight_back, valid_slots, rows_one)
+
+    tile = 2 * TILE
+    at = pl.BlockSpec((1, chans, tile), lambda w, i, p: (w, 0, i))
+    at_slot = pl.BlockSpec((1, chans, tile), lambda w, i, p: (p[w], 0, i))
+    whole = lambda rows, size: pl.BlockSpec((rows, size), lambda w, i, p: (0, 0))
+    outputs, grad_inputs = pl.pallas_call(
+        last_kernel,
+        grid_spec=pltpu.PrefetchScalarGridSpec(
+            num_scalar_prefetch=1,
+            grid=(windows, bins // tile),
+            in_specs=[
+                at, at, at_slot, at_slot,
+                pl.BlockSpec((1, 1, tile), lambda w, i, p: (w, 0, i)),
+                whole(chans, bottle), whole(8, chans), whole(8, chans), whole(1, chans),
+            ],
+            out_specs=[at, at],
+            scratch_shapes=[pltpu.VMEM((6, chans, LANES), F32), pltpu.VMEM((chans, tile), F32)],
+        ),
+        out_shape=[shape(inputs.shape, BF16), shape(inputs.shape, BF16)],
+        compiler_params=pltpu.CompilerParams(vmem_limit_bytes=40 * 1024 * 1024),
+        cost_estimate=pl.CostEstimate(flops=4 * 10**9, bytes_accessed=6 * 10**7, transcendentals=0),
+    )(
+        rank, inputs, cotangent, acts, grads, valid_rows[:, None, :], jnp.transpose(point_weight),
+        rows_one, rows_two, point_bias[None, :],
+    )
+    part = bottle // 2
+    return (
+        outputs,
+        grad_inputs,
+        rows_two[1],
+        rows_two[0],
+        conv_grad,
+        lax.dynamic_slice_in_dim(rows_one[4], side * part, part),
+        lax.dynamic_slice_in_dim(rows_one[3], side * part, part),
+        point_grad,
+        rows_one[5],
+    )
+
+
 def solution(mesh):
+    paired = mesh.shape["ch"] == 2 and mesh.shape["seq"] == 8 and mesh.shape["win"] == 2
+
+    def local(*args):
+        windows, chans, bins = args[0].shape
+        if paired and windows == 4 and chans == args[4].shape[2] and bins == 8 * TILE:
+            return local_pair(*args)
+        return local_any(*args)
+
     return jax.shard_map(
         local,
         mesh=mesh,

time: 1550 us -> 439 us (0.28)
  waiting for transfers between devices: 955 us -> 0 us
  Pallas kernels: 0 us -> 405 us
  matrix products: 194 us -> 0 us
  local copies, waits for them, and re-layouts: 160 us -> 20.2 us
  blocking collectives: 134 us -> 0 us
  other arithmetic: 80.8 us -> 8.04 us
    unnamed x5 -> x0, waiting for transfers between devices: 826 us -> none
    pallas_call x0 -> x3, Pallas kernels: none -> 405 us  [the longest x1 255 us: local_pair(): pl.pallas_call(first_kernel, in_specs=[smem, hbm, hbm, hbm, vmem, vmem, v...]
    dot_general x6 -> x0, matrix products: 194 us -> none  [the longest x1 57 us: local(): jnp.einsum('wkt,kc->wct', back_taps, back_weight, preferred_element_type=...]
    psum x4 -> x0, blocking collectives: 134 us -> none  [the longest x1 36.1 us: local(): lax.psum((sum_first, sum_second, jnp.sum(valid_rows)), ('seq', 'win'))]
    all_gather x2 -> x0, waiting for transfers between devices: 129 us -> none  [the longest x1 88.1 us: local(): complete_gradient = lax.all_gather(grad_low, 'ch', axis=1, tiled=True)]
    unnamed x55 -> x28, local copies, waits for them, and re-layouts: 76.6 us -> 10 us
    transpose x2 -> x0, local copies, waits for them, and re-layouts: 51.1 us -> none  [the longest x1 28.4 us: local(): jnp.einsum('wct,fc->wft', cotangent, point_weight, preferred_element_type...]
    convert_element_type x4 -> x3, other arithmetic: 42.4 us -> 1.51 us  [the longest x1 1.36 us: local_pair(): valid_slots = (places[None, :] < ranked[:, None]).astype(F32)]
  transfers between devices with their start and end apart: 8 -> 0, of which waited for: 3 -> 0; matrix products, arithmetic and copies ran while one was open for 18% -> 0% of each run, Pallas kernels for 0% -> 0%
where the time goes in v2:
time: 439 us; the launch traced here: 436 us
  Pallas kernels  405 us (92%)
  local copies, waits for them, and re-layouts  20.2 us (5%)
  other arithmetic  8.04 us (2%)
    pallas_call x1, Pallas kernels, local_pair(): pl.pallas_call(first_kernel, in_specs=[smem, hbm, hbm, hbm, vmem, vmem, v...  255 us
    pallas_call x1, Pallas kernels, local_pair(): pl.pallas_call(second_kernel, in_specs=[smem, hbm, hbm, hbm, hbm, hbm, hb...  123 us
    pallas_call x1, Pallas kernels, local_pair(): pl.pallas_call(last_kernel, grid_spec=pltpu.PrefetchScalarGridSpec(num_sc...  27.1 us
    unnamed x28, local copies, waits for them, and re-layouts  10 us

profile of v2, /device:TPU:0, one launch (start us, length us, event | category | flops | bytes accessed | tf_op | source)
XLA Modules:
  0.0 436.3 jit_solution(10144898790108451701)
XLA Ops:
  0.8 0.9 convert_reduce_fusion.slot
  1.7 1.3 select_reduce_fusion
  4.9 0.6 broadcast_in_dim.24
  5.6 0.6 broadcast_in_dim.25
  7.0 1.4 compare_convert_fusion.1
  8.3 1.3 clamp_reduce_fusion
  10.3 0.7 stack.18
  11.0 0.7 stack.19
  11.7 0.7 stack.20
  12.3 0.7 stack.21
  13.0 0.6 stack.23.vec
  13.6 2.4 pad_maximum_fusion.flat
  16.0 1.5 copy.31.w_mine
  17.5 255.3 %shard_map.169 = (bf16[4,384,3072]{2,1,0:T(8,128)(2,1)}, bf16[384,4992]{1,0:T(8,128)(2,1)}, bf16[384,768]{1,0:T(8,128)(2,1)}, bf16[384,384]{1,0:T(8,128)(2,1)}, ...) custom-call(s32[4]{0:T(128)} %get-tuple-element.40.order, bf16[4,384,3072]{2,1,0:T(8,128)(2,1)} %x.1, ...), custom_call_target="tpu_custom_call" | custom-call | flops 60000002048 | bytes 100000000 | tf_op jit(solution)/shard_map/pallas_call | solution.py:1254
  272.8 2.2 copy.32
  275.0 1.6 copy.33.weight
  276.6 1.0 copy-done.5
  277.6 122.7 %shard_map.170 = (bf16[4,384,3072]{2,1,0:T(8,128)(2,1)}, bf16[4,384,3072]{2,1,0:T(8,128)(2,1)}, f32[8,384]{1,0:T(8,128)S(1)}, f32[3,384,384]{2,1,0:T(8,128)}, f32[384,384]{1,0:T(8,128)S(1)}) custom-call(s32[4]{0:T(128)S(1)} %copy-done.2, bf16[4,384,3072]{2,1,0:T(8,128)(2,1)} %x.1, ...), custom_call_target="tpu_custom_call", output_to_operand_aliasing={{0}: (2, {})} | custom-call | flops 60000002048 | bytes 100000000 | tf_op jit(solution)/shard_map/pallas_call | solution.py:1310
  400.5 1.2 copy.35
  401.7 3.7 copy-done
  405.3 27.1 %shard_map.171 = (bf16[4,384,3072]{2,1,0:T(8,128)(2,1)}, bf16[4,384,3072]{2,1,0:T(8,128)(2,1)}) custom-call(s32[4]{0:T(128)S(1)} %convert_reduce_fusion.slot, bf16[4,384,3072]{2,1,0:T(8,128)(2,1)S(1)} %copy-done, bf16[4,384,3072]{2,1,0:T(8,128)(2,1)} %c.1, bf16[4,384,3072]{2,1,0:T(8,128)(2,1)} %get-tuple-element.30.act, ...), custom_call_target="tpu_custom_call" | custom-call | flops 4000000000 | bytes 60000000 | tf_op jit(solution)/shard_map/pallas_call | solution.py:1353
  433.6 0.6 constant_dynamic-slice_fusion
  434.3 1.2 copy.41
  435.5 0.8 copy.42
  (44 shorter events, 2.7 us)
Async XLA Ops:
  0.6 15.4 %copy-start.6 = (bf16[3,384,384]{2,1,0:T(8,128)(2,1)S(1)}, bf16[3,384,384]{2,1,0:T(8,128)(2,1)}, u32[]{:S(2)}) copy-start(bf16[3,384,384]{2,1,0:T(8,128)(2,1)} %param.14) | copy-start | bytes 2654212
  6.3 11.2 %copy-start.8 = (f32[1,5760]{1,0:T(1,128)}, f32[1,5760]{1,0:T(1,128)S(1)}, u32[]{:S(2)}) copy-start(f32[1,5760]{1,0:T(1,128)S(1)} %and_convert_fusion.valid_ext) | copy-start | bytes 69124
  272.8 3.8 copy-start.1
  272.8 3.8 copy-start.2
  272.8 3.8 copy-start.3
  272.8 3.8 copy-start.4
  276.6 1.0 copy-start.5
  277.6 122.7 %copy-start.9 = (s32[4]{0:T(128)S(1)}, s32[4]{0:T(128)}, u32[]{:S(2)}) copy-start(s32[4]{0:T(128)} %param.11) | copy-start | bytes 52
  277.6 124.0 %copy-start.10 = (f32[384]{0:T(512)S(1)}, f32[384]{0:T(512)}, u32[]{:S(2)}) copy-start(f32[384]{0:T(512)} %param.18) | copy-start | bytes 4612
  401.6 3.7 copy-start
  405.3 28.9 %copy-start.7 = (f32[3,384,384]{2,1,0:T(8,128)S(1)}, f32[3,384,384]{2,1,0:T(8,128)}, u32[]{:S(2)}) copy-start(f32[3,384,384]{2,1,0:T(8,128)} %get-tuple-element.65) | copy-start | bytes 5308420

commit v3 on v2

--- a/solution.py
+++ b/solution.py
@@ -312,12 +312,58 @@
 A_MINE, B_MINE, A_OTHER, B_OTHER, MEAN, SCALE, GAIN, OFFSET, FACTOR, BETA, GAMMA = range(11)
 
 
+class Order:
+    def __init__(self, lengths):
+        self.lengths = [lengths[i] for i in range(4)]
+        ranks = []
+        for i, mine in enumerate(self.lengths):
+            rank = jnp.int32(0)
+            for j, their in enumerate(self.lengths):
+                if j < i:
+                    rank = rank + jnp.where(their >= mine, 1, 0)
+                elif j > i:
+                    rank = rank + jnp.where(their > mine, 1, 0)
+            ranks.append(rank)
+
+        def at_slot(slot, values):
+            found = jnp.int32(0)
+            for rank, value in zip(ranks, values, strict=True):
+                found = found + jnp.where(rank == slot, value, 0)
+            return found
+
+        self.windows = [at_slot(slot, range(4)) for slot in range(4)]
+        self.sizes = [at_slot(slot, self.lengths) for slot in range(4)]
+
+    def of(self, values, slot):
+        if isinstance(slot, int):
+            return values[slot]
+        found = values[0]
+        for at in range(1, 4):
+            found = jnp.where(slot == at, values[at], found)
+        return found
+
+    def __getitem__(self, slot):
+        return self.of(self.windows, slot)
+
+    def size(self, slot):
+        return self.of(self.sizes, slot)
+
+
+def valid_lanes(start, size, limit):
+    spots = start + lax.broadcasted_iota(jnp.int32, (1, size), 1)
+    return ((spots >= 0) & (spots < limit)).astype(F32)
+
+
+def as_row(ref):
+    return ref[...].reshape(1, ref.shape[0])
+
+
 def first_kernel(
-    order, xin, cin, flat, w_mine, point, valid_rows, valid_ext, valid_own, vec,
+    lengths, xin, cin, weight_hbm, point_hbm, weight, point, gains_in, offsets_in, gains_mid, offsets_mid,
     acts, g_own, g_two, g_extra, gw, gp, rows_out,
     xbuf, p1a, p2a, p1b, p2b, qext, ex, ec, halo_r, halo_l, hb,
     act_m, act_o, conv, actm, gco, w_all, w_other, e_act, cat, tmp, acc1, acc2, cols,
-    msg, slots, ymsg, yin, send, recv,
+    msg, slots, ymsg, yin, valid_rows, valid_ext, valid_own, send, recv,
 ):
     place = Place()
     side, group, core, partner = place.side, place.group, place.core, place.partner
@@ -328,6 +374,7 @@
     base2, base3 = bins + 2 * LANES, bins + half + 4 * LANES
     own2, own3 = bins, bins + half
     low = lax.broadcasted_iota(jnp.int32, (ROWS, LANES), 1) < LANES // 2
+    order = Order(lengths)
 
     def put_rows(dst, at, load, size):
         def body(rows):
@@ -350,17 +397,31 @@
         pl.multiple_of((w * 8 + c * 4 + z) * share, share), size * share
     )
     mine_at = share_rows(place.win, core, group)
-    w_first = copies.remote(flat.at[mine_at], w_other.at[mine_at], partner)
-    w_first.start()
+    share_at = place.win * 8 + core * 4 + group
+    taps, conv_shares = weight.shape[0], weight.shape[0] * chans // share
+    per_tap = chans // share
+    w_at = copies.take()
+    w_tap = copies.remote(
+        weight_hbm.at[jnp.minimum(share_at // per_tap, taps - 1), pl.ds(pl.multiple_of(share_at % per_tap * share, share), share)],
+        w_other.at[mine_at], partner, w_at, w_at,
+    )
+    w_point = copies.remote(
+        point_hbm.at[pl.ds(pl.multiple_of(share_at % per_tap * share, share), share)],
+        w_other.at[mine_at], partner, w_at, w_at,
+    )
+    w_first = w_point
+    pl.when(share_at < conv_shares)(w_tap.start)
+    pl.when(share_at >= conv_shares)(w_point.start)
     for copy in loads:
         copy.wait()
-    put_rows(p1a, 0, lambda rows: xbuf[order[other], rows, :], bins)
     x1 = [
         copies.remote(p1a.at[:, i * chunk : (i + 1) * chunk], p2a.at[:, i * chunk : (i + 1) * chunk], partner)
         for i in range(4)
     ]
-    x1[0].start()
-    x1[1].start()
+    for i in range(4):
+        put_rows(p1a, i * chunk, lambda rows, i=i: xbuf[order[other], rows, i * chunk : (i + 1) * chunk], chunk)
+        if i < 2:
+            x1[i].start()
     to_left = copies.remote(xbuf.at[:, :, 0:LANES], halo_r, {"seq": jnp.maximum(place.shard - 1, 0)})
     to_right = copies.remote(xbuf.at[:, :, bins - LANES : bins], halo_l, {"seq": jnp.minimum(place.shard + 1, 7)})
     pl.when(place.shard > 0)(to_left.start)
@@ -374,6 +435,23 @@
     def _():
         halo_r[...] = jnp.zeros_like(halo_r)
 
+    for w in range(windows):
+        valid_rows[w : w + 1, :] = valid_lanes(place.shard * bins, bins, order.lengths[w])
+    at = 0
+    for start, size, limit in (
+        (place.shard * bins, bins, order.size(side)),
+        (place.shard * bins + side * half, half, order.size(2)),
+        (core * bins + group * piece + side * eighth, eighth, order.size(3)),
+    ):
+        valid_ext[:, at : at + size + 2 * LANES] = valid_lanes(start - LANES, size + 2 * LANES, limit)
+        at += size + 2 * LANES
+    for to, at, size in ((0, LANES, bins), (own2, base2 + LANES, half), (own3, base3 + LANES, eighth)):
+        valid_own[:, to : to + size] = valid_ext[:, at : at + size]
+    count = jnp.int32(0)
+    for length in order.lengths:
+        count = count + jnp.clip(length - place.shard * bins, 0, bins)
+    count_row = jnp.full((1, chans), count, jnp.int32).astype(F32)
+    gain_in, offset_in = as_row(gains_in), as_row(offsets_in)
     acc1[...] = jnp.zeros_like(acc1)
     acc2[...] = jnp.zeros_like(acc2)
     for w in range(windows):
@@ -391,13 +469,14 @@
         by_rows(chans, body)
     plane = [PlaneSum(copies, place, msg.at[i], slots.at[i]) for i in range(3)]
     over_y = [copies.remote(ymsg.at[i], yin.at[i], partner) for i in range(3)]
-    plane[0].start([to_row(acc1[...]), to_row(acc2[...]), vec[4:5, :]])
+    plane[0].start([to_row(acc1[...]), to_row(acc2[...]), count_row])
 
     put_rows(qext, LANES, lambda rows: xbuf[order[3], rows, :], bins)
-    w_all[:, : 3 * chans] = w_mine[...]
+    for tap in range(3):
+        w_all[:, tap * chans : (tap + 1) * chans] = jnp.transpose(weight[tap])
     total = plane[0].finish()
     filled = total[2:3, :]
-    ymsg[0] = jnp.concatenate([total[0:3, :], vec[0:2, :], total[0:3, :]], axis=0)
+    ymsg[0] = jnp.concatenate([total[0:3, :], gain_in, offset_in, total[0:3, :]], axis=0)
     over_y[0].start()
     x1[2].start()
     x1[3].start()
@@ -407,14 +486,15 @@
         scale = lax.rsqrt(second / filled - mean * mean + EPS)
         return mean, scale, scale * gain, offset - mean * scale * gain
 
-    mean, scale, a_mine, b_mine = norm_of(total[0:1, :], total[1:2, :], vec[0:1, :], vec[1:2, :])
+    mean, scale, a_mine, b_mine = norm_of(total[0:1, :], total[1:2, :], gain_in, offset_in)
     column(A_MINE, a_mine)
     column(B_MINE, b_mine)
     rows_out[...] = jnp.zeros_like(rows_out)
     rows_out[0:1, :] = mean
     rows_out[1:2, :] = scale
     rows_out[2:3, :] = filled
-    rows_out[6:8, :] = vec[0:2, :]
+    rows_out[6:7, :] = gain_in
+    rows_out[7:8, :] = offset_in
 
     w_first.wait_recv()
     z_first = copies.take(4)
@@ -578,19 +658,6 @@
     for copy in cot_loads:
         copy.wait()
     put_rows(p2a, 0, lambda rows: xbuf[order[other], rows, :], bins)
-
-    @pl.when(group == 0)
-    def _():
-        for copy in ex_out:
-            copy.wait_send()
-
-    put_rows(qext, LANES, lambda rows: xbuf[order[3], rows, :], bins)
-
-    @pl.when(group == 0)
-    def _():
-        for copy in ec_out:
-            copy.start()
-        put_rows(ec, 0, lambda rows: qext[rows, LANES : LANES + piece], piece)
 
     def fill_taps(start):
         for at_half, ref in enumerate((act_m, act_o)):
@@ -659,9 +726,20 @@
     ymsg[1] = total
     over_y[1].start()
     c1[3].start()
-    pl.when(group > 0)(lambda: ec_out[0].wait_recv())
+
+    @pl.when(group == 0)
+    def _():
+        for copy in ex_out:
+            copy.wait_send()
+
+    put_rows(qext, LANES, lambda rows: xbuf[order[3], rows, :], bins)
+
+    @pl.when(group == 0)
+    def _():
+        for copy in ec_out:
+            copy.start()
+        put_rows(ec, 0, lambda rows: qext[rows, LANES : LANES + piece], piece)
     put_rows(p2b, 0, lambda rows: xbuf[order[2], rows, lanes_at(other * half, half)], half)
-    put_rows(p2b, half, lambda rows: ec[rows, lanes_at(other * eighth, eighth)], eighth)
     cuts = (0, half // 2, half, half + eighth)
     c2 = [copies.remote(p2b.at[:, lo:hi], p1b.at[:, lo:hi], partner) for lo, hi in zip(cuts, cuts[1:])]
     c1[2].wait_recv()
@@ -669,7 +747,7 @@
 
     over_y[1].wait_recv()
     total = ymsg[1] + yin[1]
-    gain_mid, offset_mid = vec[2:3, :], vec[3:4, :]
+    gain_mid, offset_mid = as_row(gains_mid), as_row(offsets_mid)
     mean = total[0:1, :] / filled
     scale = lax.rsqrt(total[1:2, :] / filled - mean * mean + EPS)
     for at, row in ((MEAN, mean), (SCALE, scale), (GAIN, gain_mid), (OFFSET, offset_mid), (FACTOR, gain_mid * scale)):
@@ -687,6 +765,19 @@
         by_rows(chans, body)
 
     times(conv.shape[1] // TILE, act_tile)
+    back_to = {"seq": core}
+    e_at = copies.take(8)
+    e_parts = ((actm.at[:, own3:], side), (e_act, other))
+    e_home = [
+        copies.remote(
+            src, acts.at[3, :, lanes_at(group * piece + role * eighth, eighth)], back_to,
+            e_at + which, e_at + 2 * group + which,
+        )
+        for which, (src, role) in enumerate(e_parts)
+    ]
+    e_mine = [copies.local(src, acts.at[3, :, lanes_at(role * eighth, eighth)]) for src, role in e_parts]
+    pl.when(group > 0)(e_home[0].start)
+    pl.when(group == 0)(e_mine[0].start)
     keeps = [
         copies.local(actm.at[:, 0:bins], acts.at[side]),
         copies.local(actm.at[:, own2:own3], acts.at[2, :, lanes_at(side * half, half)]),
@@ -766,8 +857,10 @@
             c1[i].wait_recv()
         if i == 3:
             c2[1].start()
-            c2[2].start()
         over_first(sum_tile, i * chunk, (i + 1) * chunk)
+    pl.when(group > 0)(lambda: ec_out[0].wait_recv())
+    put_rows(p2b, half, lambda rows: ec[rows, lanes_at(other * eighth, eighth)], eighth)
+    c2[2].start()
     c2[0].wait_recv()
     over_second(sum_tile, 0, half // 2)
     c2[1].wait_recv()
@@ -782,6 +875,9 @@
     over_y[2].start()
     for copy in t3[1:]:
         copy.start()
+    t3_extra.wait_recv()
+    pl.when(group > 0)(e_home[1].start)
+    pl.when(group == 0)(e_mine[1].start)
     over_y[2].wait_recv()
     beta = ymsg[2, 0:1, :] + yin[2, 0:1, :]
     gamma = ymsg[2, 1:2, :] + yin[2, 1:2, :]
@@ -802,31 +898,6 @@
     g_keep = copies.local(gco, g_own)
     g_keep.start()
 
-    back_to = {"seq": core}
-    e_at = copies.take(8)
-    t3_extra.wait_recv()
-    e_home = [
-        copies.remote(
-            src, acts.at[3, :, lanes_at(group * piece + role * eighth, eighth)], back_to,
-            e_at + which, e_at + 2 * group + which,
-        )
-        for which, (src, role) in enumerate(((actm.at[:, own3:], side), (e_act, other)))
-    ]
-    e_mine = [
-        copies.local(src, acts.at[3, :, lanes_at(role * eighth, eighth)])
-        for src, role in ((actm.at[:, own3:], side), (e_act, other))
-    ]
-
-    @pl.when(group > 0)
-    def _():
-        for copy in e_home:
-            copy.start()
-
-    @pl.when(group == 0)
-    def _():
-        for copy in e_mine:
-            copy.start()
-
     weight_sum = conv.at[:, 0 : 6 * chans]
     weight_sum[...] = jnp.zeros_like(weight_sum)
 
@@ -871,10 +942,10 @@
 
 
 def second_kernel(
-    order, xin, acts_in, g_own, g_two, g_extra, gw, gp, weight, valid, rows_in,
+    lengths, xin, acts_in, g_own, g_two, g_extra, gw, gp, weights, rows_in,
     acts, grads, rows_out, conv_grad, point_grad,
     gs, xbuf, halo_r, halo_l, cat, tmp, acc1, acc2, cols, msg, slots,
-    parts, parts_core, parts_win, parts_z, parts_side, summed, send, recv,
+    parts, parts_core, parts_win, parts_z, parts_side, summed, weight, send, recv,
 ):
     del acts_in
     place = Place()
@@ -1024,6 +1095,9 @@
         for copy in e_home:
             copy.start()
 
+    order = Order(lengths)
+    for tap in range(weights.shape[0]):
+        weight[:, tap * chans : (tap + 1) * chans] = weights[tap]
     names = {"mean": 0, "scale": 1, "gain": 2, "offset": 3}
     for at, row in enumerate((0, 1, 6, 7)):
         cols[at] = to_column(rows_in[row : row + 1, :])
@@ -1039,7 +1113,7 @@
                 cat[tap * chans : (tap + 1) * chans, :] = cells[:, at : at + TILE]
             tmp[...] = dot(weight[...], cat[...])
             at = lanes_at(i * TILE, TILE)
-            mask = valid[pl.ds(slot, 1), at]
+            mask = valid_lanes(place.shard * bins + i * TILE, TILE, order.size(slot))
             window = order[slot]
 
             def body(rows):
@@ -1151,29 +1225,50 @@
         copy.wait_recv()
 
 
-def last_kernel(slot, x, c, act, grad, valid, weight, rows_one, rows_two, bias, out, grad_out, cols, tmp):
-    del slot
-
-    @pl.when((pl.program_id(0) == 0) & (pl.program_id(1) == 0))
+def last_kernel(
+    lengths, x, c, act, grad, point, bias, rows_one, rows_two, conv_in, point_in,
+    out, grad_out, gain_in, offset_in, gain_mid, offset_mid, grad_bias, conv_out, point_out,
+    weight, cols, tmp,
+):
+    window, tile = pl.program_id(0), pl.program_id(1)
+    side, shard = lax.axis_index("ch"), lax.axis_index("seq")
+    conv_out[...] = conv_in[...]
+    point_out[...] = point_in[...]
+
+    @pl.when((window == 0) & (tile == 0))
     def _():
+        weight[...] = jnp.transpose(point[...])
         mean, scale, filled, gain = (rows_one[i : i + 1, :] for i in (0, 1, 2, 6))
+        beta, gamma = rows_two[0:1, :], rows_two[1:2, :]
+        factor = gain * scale
+        slope = factor * scale * gamma / filled
         for at, row in enumerate(
-            (mean, scale, gain * scale, rows_two[0:1, :] / filled, rows_two[1:2, :] / filled, bias[...])
+            (factor, slope, factor * beta / filled - mean * slope, bias[...].reshape(beta.shape))
         ):
             cols[at] = to_column(row)
-
-    mask = valid[0] > 0.0
+        size = gain_in.shape[0]
+        gain_in[...] = gamma.reshape(size)
+        offset_in[...] = beta.reshape(size)
+        grad_bias[...] = rows_one[5:6, :].reshape(size)
+        part = size // 2
+        for ref, row in ((gain_mid, rows_one[4:5, :]), (offset_mid, rows_one[3:4, :])):
+            ref[...] = jnp.where(side == 0, row[:, :part], row[:, part:])
+
     size = x.shape[2]
-    cells = jnp.where(mask, act[0].astype(F32), 0.0).astype(BF16)
-    tmp[...] = dot(weight[...], cells)
-    wide = lambda at, rows: spread_lanes(cols[at, rows, :], size)
-
+    bins = pl.num_programs(1) * size
+    mask = valid_lanes(shard * bins + tile * size, size, lengths[window]) > 0.0
+    tmp[...] = dot(weight[...], act[0])
     def body(rows):
-        xs = x[0, rows, :].astype(F32)
-        out[0, rows, :] = (xs + tmp[rows, :] + wide(5, rows)).astype(BF16)
-        norm = (xs - wide(0, rows)) * wide(1, rows)
-        back = wide(2, rows) * (grad[0, rows, :].astype(F32) - (wide(3, rows) + norm * wide(4, rows)))
-        grad_out[0, rows, :] = (c[0, rows, :].astype(F32) + jnp.where(mask, back, 0.0)).astype(BF16)
+        factor, slope, shift, more = (spread_lanes(cols[i, rows, :], TILE) for i in range(4))
+        for at in range(0, size, TILE):
+            lanes = slice(at, at + TILE)
+            kept = mask[:, lanes]
+            xs = x[0, rows, lanes].astype(F32)
+            out[0, rows, lanes] = (xs + jnp.where(kept, tmp[rows, lanes], 0.0) + more).astype(BF16)
+            back = factor * grad[0, rows, lanes].astype(F32) - xs * slope - shift
+            grad_out[0, rows, lanes] = (
+                c[0, rows, lanes].astype(F32) + jnp.where(kept, back, 0.0)
+            ).astype(BF16)
 
     by_rows(x.shape[1], body)
 
@@ -1192,68 +1287,16 @@
 ):
     windows, chans, bins = inputs.shape
     taps, _, bottle = conv_weight.shape
-    side, shard, _ = (lax.axis_index(name) for name in ("ch", "seq", "win"))
-    group = shard // 2
     piece, half, eighth = bins // 4, bins // 2, bins // 8
     widened, packed = bins + half + eighth + 6 * LANES, bins + half + eighth
 
-    ids = jnp.arange(windows, dtype=jnp.int32)
-    ahead = (lengths[None, :] > lengths[:, None]) | (
-        (lengths[None, :] == lengths[:, None]) & (ids[None, :] < ids[:, None])
-    )
-    rank = jnp.sum(ahead.astype(jnp.int32), axis=1)
-    chosen = rank[None, :] == ids[:, None]
-    order = jnp.sum(jnp.where(chosen, ids[None, :], 0), axis=1)
-    ranked = jnp.sum(jnp.where(chosen, lengths[None, :], 0), axis=1)
-
-    places = shard * bins + jnp.arange(bins, dtype=jnp.int32)
-    valid_rows = (places[None, :] < lengths[:, None]).astype(F32)
-    valid_slots = (places[None, :] < ranked[:, None]).astype(F32)
-    starts = (
-        shard * bins,
-        shard * bins + side * half,
-        (shard % 2) * bins + group * piece + side * eighth,
-    )
-    limits = (jnp.where(side == 0, ranked[0], ranked[1]), ranked[2], ranked[3])
-    spots = jnp.concatenate(
-        [
-            at - LANES + jnp.arange(size + 2 * LANES, dtype=jnp.int32)
-            for at, size in zip(starts, (bins, half, eighth), strict=True)
-        ]
-    )
-    limit = jnp.concatenate(
-        [
-            jnp.full((size + 2 * LANES,), at, jnp.int32)
-            for at, size in zip(limits, (bins, half, eighth), strict=True)
-        ]
-    )
-    valid_ext = ((spots >= 0) & (spots < limit)).astype(F32)[None, :]
-    valid_own = jnp.concatenate(
-        [
-            valid_ext[:, at : at + size]
-            for at, size in (
-                (LANES, bins),
-                (bins + 3 * LANES, half),
-                (bins + half + 5 * LANES, eighth),
-            )
-        ],
-        axis=1,
-    )
-    kept = jnp.sum(jnp.clip(lengths - shard * bins, 0, bins)).astype(F32)
-    zero = jnp.zeros((chans,), F32)
-    vec = jnp.stack(
-        [gain_in, offset_in, gain_mid, offset_mid, jnp.full((chans,), kept), zero, zero, zero]
-    )
-    turn = lambda w: jnp.transpose(w, (2, 0, 1)).reshape(bottle, taps * chans)
-    flat = jnp.concatenate([conv_weight.reshape(taps * chans, bottle), point_weight], axis=0)
-
     vmem = pl.BlockSpec(memory_space=pltpu.VMEM)
-    hbm = pl.BlockSpec(memory_space=pl.ANY)
+    hbm = pl.BlockSpec(memory_space=pltpu.HBM)
     smem = pl.BlockSpec(memory_space=pltpu.SMEM)
     shape = jax.ShapeDtypeStruct
     acts, g_own, g_two, g_extra, gw, gp, rows_one = pl.pallas_call(
         first_kernel,
-        in_specs=[smem, hbm, hbm, hbm, vmem, vmem, vmem, vmem, vmem, vmem],
+        in_specs=[smem, hbm, hbm, hbm, hbm, vmem, vmem, vmem, vmem, vmem, vmem],
         out_specs=[hbm, hbm, hbm, hbm, hbm, vmem, vmem],
         out_shape=[
             shape((windows, bottle, bins), BF16),
@@ -1293,6 +1336,9 @@
             pltpu.VMEM((3, PLANE, 8, chans), F32),
             pltpu.VMEM((3, 8, chans), F32),
             pltpu.VMEM((3, 8, chans), F32),
+            pltpu.VMEM((windows, bins), F32),
+            pltpu.VMEM((1, widened), F32),
+            pltpu.VMEM((1, packed), F32),
             pltpu.SemaphoreType.DMA((128,)),
             pltpu.SemaphoreType.DMA((128,)),
         ],
@@ -1301,15 +1347,14 @@
         ),
         cost_estimate=pl.CostEstimate(flops=60 * 10**9, bytes_accessed=10**8, transcendentals=0),
     )(
-        order, inputs, cotangent, flat, turn(conv_weight), point_weight,
-        valid_rows, valid_ext, valid_own, vec,
-    )
-
-    weight_back = jnp.transpose(conv_weight, (1, 0, 2)).reshape(chans, taps * bottle)
+        lengths, inputs, cotangent, conv_weight, point_weight, conv_weight, point_weight,
+        gain_in, offset_in, gain_mid, offset_mid,
+    )
+
     share = bottle // PLANE
     acts, grads, rows_two, conv_grad, point_grad = pl.pallas_call(
         second_kernel,
-        in_specs=[smem, hbm, hbm, hbm, hbm, hbm, hbm, hbm, vmem, vmem, vmem],
+        in_specs=[smem, hbm, hbm, hbm, hbm, hbm, hbm, hbm, vmem, vmem],
         out_specs=[hbm, hbm, vmem, vmem, vmem],
         out_shape=[
             shape((windows, bottle, bins), BF16),
@@ -1337,50 +1382,79 @@
             pltpu.VMEM((4, 2, share, (taps + 1) * chans), F32),
             pltpu.VMEM((share, (taps + 1) * chans), F32),
             pltpu.VMEM((bottle, (taps + 1) * chans), F32),
+            pltpu.VMEM((chans, taps * bottle), BF16),
             pltpu.SemaphoreType.DMA((128,)),
             pltpu.SemaphoreType.DMA((128,)),
         ],
         compiler_params=pltpu.CompilerParams(
-            collective_id=1, has_side_effects=True, vmem_limit_bytes=52 * 1000 * 1000
+            collective_id=1, has_side_effects=True, vmem_limit_bytes=VMEM_BYTES
         ),
         cost_estimate=pl.CostEstimate(flops=60 * 10**9, bytes_accessed=10**8, transcendentals=0),
-    )(order, inputs, acts, g_own, g_two, g_extra, gw, gp, weight_back, valid_slots, rows_one)
-
-    tile = 2 * TILE
+    )(lengths, inputs, acts, g_own, g_two, g_extra, gw, gp, conv_weight, rows_one)
+
+    def slot_of(window, sizes):
+        rank = jnp.int32(0)
+        for other in range(windows):
+            longer = sizes[other] > sizes[window]
+            ahead = (sizes[other] == sizes[window]) & (other < window)
+            rank = rank + jnp.where(longer | ahead, 1, 0)
+        return rank
+
+    tile = bins
     at = pl.BlockSpec((1, chans, tile), lambda w, i, p: (w, 0, i))
-    at_slot = pl.BlockSpec((1, chans, tile), lambda w, i, p: (p[w], 0, i))
+    at_slot = pl.BlockSpec((1, chans, tile), lambda w, i, p: (slot_of(w, p), 0, i))
     whole = lambda rows, size: pl.BlockSpec((rows, size), lambda w, i, p: (0, 0))
-    outputs, grad_inputs = pl.pallas_call(
+    steps = bins // tile
+    part = chans // (windows * steps)
+    conv_at = pl.BlockSpec((taps, part, bottle), lambda w, i, p: (0, w * steps + i, 0))
+    point_at = pl.BlockSpec((part, chans), lambda w, i, p: (w * steps + i, 0))
+    line = lambda size: pl.BlockSpec((size,), lambda w, i, p: (0,))
+    outputs, grad_inputs, gamma_in, beta_in, gamma_mid, beta_mid, grad_bias, conv_grad, point_grad = pl.pallas_call(
         last_kernel,
         grid_spec=pltpu.PrefetchScalarGridSpec(
             num_scalar_prefetch=1,
             grid=(windows, bins // tile),
             in_specs=[
                 at, at, at_slot, at_slot,
-                pl.BlockSpec((1, 1, tile), lambda w, i, p: (w, 0, i)),
-                whole(chans, bottle), whole(8, chans), whole(8, chans), whole(1, chans),
+                whole(bottle, chans), line(chans), whole(8, chans), whole(8, chans), conv_at, point_at,
             ],
-            out_specs=[at, at],
-            scratch_shapes=[pltpu.VMEM((6, chans, LANES), F32), pltpu.VMEM((chans, tile), F32)],
+            out_specs=[
+                at, at, line(chans), line(chans), whole(1, bottle // 2), whole(1, bottle // 2),
+                line(chans), conv_at, point_at,
+            ],
+            scratch_shapes=[
+                pltpu.VMEM((chans, bottle), BF16),
+                pltpu.VMEM((4, chans, LANES), F32),
+                pltpu.VMEM((chans, tile), F32),
+            ],
         ),
-        out_shape=[shape(inputs.shape, BF16), shape(inputs.shape, BF16)],
-        compiler_params=pltpu.CompilerParams(vmem_limit_bytes=40 * 1024 * 1024),
+        out_shape=[
+            shape(inputs.shape, BF16),
+            shape(inputs.shape, BF16),
+            shape((chans,), F32),
+            shape((chans,), F32),
+            shape((1, bottle // 2), F32),
+            shape((1, bottle // 2), F32),
+            shape((chans,), F32),
+            shape((taps, chans, bottle), F32),
+            shape((bottle, chans), F32),
+        ],
+        compiler_params=pltpu.CompilerParams(vmem_limit_bytes=VMEM_BYTES),
         cost_estimate=pl.CostEstimate(flops=4 * 10**9, bytes_accessed=6 * 10**7, transcendentals=0),
     )(
-        rank, inputs, cotangent, acts, grads, valid_rows[:, None, :], jnp.transpose(point_weight),
-        rows_one, rows_two, point_bias[None, :],
-    )
-    part = bottle // 2
+        lengths, inputs, cotangent, acts, grads, point_weight, point_bias, rows_one, rows_two,
+        conv_grad, point_grad,
+    )
     return (
         outputs,
         grad_inputs,
-        rows_two[1],
-        rows_two[0],
+        gamma_in,
+        beta_in,
         conv_grad,
-        lax.dynamic_slice_in_dim(rows_one[4], side * part, part),
-        lax.dynamic_slice_in_dim(rows_one[3], side * part, part),
+        gamma_mid[0],
+        beta_mid[0],
         point_grad,
-        rows_one[5],
+        grad_bias,
     )
 
 

time: 439 us -> 393 us (0.90)
  local copies, waits for them, and re-layouts: 20.2 us -> 0 us
  Pallas kernels: 405 us -> 391 us
  other arithmetic: 8.04 us -> 0 us
    pallas_call x1, Pallas kernels: 255 us -> 237 us  [local_pair(): pl.pallas_call(first_kernel, in_specs=[smem, hbm, hbm, hbm, hbm, vmem, vm...]
    unnamed x28 -> x0, local copies, waits for them, and re-layouts: 10 us -> none
    pallas_call x1, Pallas kernels: 123 us -> 128 us  [local_pair(): pl.pallas_call(second_kernel, in_specs=[smem, hbm, hbm, hbm, hbm, hbm, hb...]
where the time goes in v3:
time: 393 us; the launch traced here: 392 us
  Pallas kernels  391 us (99%)
    pallas_call x1, Pallas kernels, local_pair(): pl.pallas_call(first_kernel, in_specs=[smem, hbm, hbm, hbm, hbm, vmem, vm...  237 us
    pallas_call x1, Pallas kernels, local_pair(): pl.pallas_call(second_kernel, in_specs=[smem, hbm, hbm, hbm, hbm, hbm, hb...  128 us
    pallas_call x1, Pallas kernels, local_pair(): pl.pallas_call(last_kernel, grid_spec=pltpu.PrefetchScalarGridSpec(num_sc...  26.2 us

profile of v3, /device:TPU:0, one launch (start us, length us, event | category | flops | bytes accessed | tf_op | source)
XLA Modules:
  0.0 392.0 jit_solution(15985663075336410451)
XLA Ops:
  0.6 237.1 %shard_map.169 = (bf16[4,384,3072]{2,1,0:T(8,128)(2,1)}, bf16[384,4992]{1,0:T(8,128)(2,1)}, bf16[384,768]{1,0:T(8,128)(2,1)}, bf16[384,384]{1,0:T(8,128)(2,1)}, ...) custom-call(s32[4]{0:T(128)} %lengths.5, bf16[4,384,3072]{2,1,0:T(8,128)(2,1)} %x.1, ...), custom_call_target="tpu_custom_call" | custom-call | flops 60000002048 | bytes 100000000 | tf_op jit(solution)/shard_map/pallas_call | solution.py:1297
  237.8 127.8 %shard_map.170 = (bf16[4,384,3072]{2,1,0:T(8,128)(2,1)}, bf16[4,384,3072]{2,1,0:T(8,128)(2,1)}, f32[8,384]{1,0:T(8,128)}, f32[3,384,384]{2,1,0:T(8,128)}, f32[384,384]{1,0:T(8,128)}) custom-call(s32[4]{0:T(128)} %lengths.5, bf16[4,384,3072]{2,1,0:T(8,128)(2,1)} %x.1, ...), custom_call_target="tpu_custom_call", output_to_operand_aliasing={{0}: (2, {})} | custom-call | flops 60000002048 | bytes 100000000 | tf_op jit(solution)/shard_map/pallas_call | solution.py:1355
  365.6 26.2 %shard_map.171 = (bf16[4,384,3072]{2,1,0:T(8,128)(2,1)}, bf16[4,384,3072]{2,1,0:T(8,128)(2,1)}, f32[384]{0:T(512)}, f32[384]{0:T(512)}, f32[1,192]{1,0:T(1,128)}...) custom-call(s32[4]{0:T(128)} %lengths.5, bf16[4,384,3072]{2,1,0:T(8,128)(2,1)} %x.1, ...), custom_call_target="tpu_custom_call" | custom-call | flops 4000000000 | bytes 60000000 | tf_op jit(solution)/shard_map/pallas_call | solution.py:1412

commit v4 on v3

--- a/solution.py
+++ b/solution.py
@@ -209,7 +209,7 @@
         body(pl.ds(pl.multiple_of(i * ROWS, ROWS), ROWS))
         return carry
 
-    lax.fori_loop(0, count // ROWS, step, 0)
+    lax.fori_loop(0, count // ROWS, step, 0, unroll=3)
 
 
 def times(count, body):

time: 393 us -> 390 us (level)
  no operation moved by 1% of the time
where the time goes in v4:
time: 390 us; the launch traced here: 389 us
  Pallas kernels  389 us (100%)
    pallas_call x1, Pallas kernels, local_pair(): pl.pallas_call(first_kernel, in_specs=[smem, hbm, hbm, hbm, hbm, vmem, vm...  237 us
    pallas_call x1, Pallas kernels, local_pair(): pl.pallas_call(second_kernel, in_specs=[smem, hbm, hbm, hbm, hbm, hbm, hb...  125 us
    pallas_call x1, Pallas kernels, local_pair(): pl.pallas_call(last_kernel, grid_spec=pltpu.PrefetchScalarGridSpec(num_sc...  26 us

profile of v4, /device:TPU:0, one launch (start us, length us, event | category | flops | bytes accessed | tf_op | source)
XLA Modules:
  0.0 389.4 jit_solution(3186822199714171001)
XLA Ops:
  0.6 237.1 %shard_map.169 = (bf16[4,384,3072]{2,1,0:T(8,128)(2,1)}, bf16[384,4992]{1,0:T(8,128)(2,1)}, bf16[384,768]{1,0:T(8,128)(2,1)}, bf16[384,384]{1,0:T(8,128)(2,1)}, ...) custom-call(s32[4]{0:T(128)} %lengths.5, bf16[4,384,3072]{2,1,0:T(8,128)(2,1)} %x.1, ...), custom_call_target="tpu_custom_call" | custom-call | flops 60000002048 | bytes 100000000 | tf_op jit(solution)/shard_map/pallas_call | solution.py:1297
  237.8 125.4 %shard_map.170 = (bf16[4,384,3072]{2,1,0:T(8,128)(2,1)}, bf16[4,384,3072]{2,1,0:T(8,128)(2,1)}, f32[8,384]{1,0:T(8,128)}, f32[3,384,384]{2,1,0:T(8,128)}, f32[384,384]{1,0:T(8,128)}) custom-call(s32[4]{0:T(128)} %lengths.5, bf16[4,384,3072]{2,1,0:T(8,128)(2,1)} %x.1, ...), custom_call_target="tpu_custom_call", output_to_operand_aliasing={{0}: (2, {})} | custom-call | flops 60000002048 | bytes 100000000 | tf_op jit(solution)/shard_map/pallas_call | solution.py:1355
  363.2 26.0 %shard_map.171 = (bf16[4,384,3072]{2,1,0:T(8,128)(2,1)}, bf16[4,384,3072]{2,1,0:T(8,128)(2,1)}, f32[384]{0:T(512)}, f32[384]{0:T(512)}, f32[1,192]{1,0:T(1,128)}...) custom-call(s32[4]{0:T(128)} %lengths.5, bf16[4,384,3072]{2,1,0:T(8,128)(2,1)} %x.1, ...), custom_call_target="tpu_custom_call" | custom-call | flops 4000000000 | bytes 60000000 | tf_op jit(solution)/shard_map/pallas_call | solution.py:1412

commit v5 on v4

--- a/solution.py
+++ b/solution.py
@@ -1,3 +1,5 @@
+import functools
+
 import jax
 import jax.numpy as jnp
 from jax import lax
@@ -209,7 +211,7 @@
         body(pl.ds(pl.multiple_of(i * ROWS, ROWS), ROWS))
         return carry
 
-    lax.fori_loop(0, count // ROWS, step, 0, unroll=3)
+    lax.fori_loop(0, count // ROWS, step, 0, unroll=6)
 
 
 def times(count, body):
@@ -890,10 +892,10 @@
     over_third(grad_tile)
     t4_extra = copies.remote(gco.at[:, own3:], g_extra, partner)
     t4_extra.start()
-    over_second(grad_tile, 0, half // 2)
-    t4 = copies.remote(gco.at[:, own2 : own2 + half // 2], g_two, partner)
+    over_second(grad_tile, 0, half // 4)
+    t4 = copies.remote(gco.at[:, own2 : own2 + half // 4], g_two, partner)
     t4.start()
-    over_second(grad_tile, half // 2, half)
+    over_second(grad_tile, half // 4, half)
     over_first(grad_tile, 0, bins)
     g_keep = copies.local(gco, g_own)
     g_keep.start()
@@ -942,9 +944,9 @@
 
 
 def second_kernel(
-    lengths, xin, acts_in, g_own, g_two, g_extra, gw, gp, weights, rows_in,
+    lengths, xin, cin, acts_in, g_own, g_two, g_extra, gw, gp, weights, rows_in,
     acts, grads, rows_out, conv_grad, point_grad,
-    gs, xbuf, halo_r, halo_l, cat, tmp, acc1, acc2, cols, msg, slots,
+    gs, xbuf, cbuf, halo_r, halo_l, cat, tmp, acc1, acc2, cols, msg, slots,
     parts, parts_core, parts_win, parts_z, parts_side, summed, weight, send, recv,
 ):
     del acts_in
@@ -959,7 +961,7 @@
     own_loads = [
         copies.local(g_own.at[:, 0:bins], gs.at[side, :, LANES : LANES + bins]),
         copies.local(g_own.at[:, own2:own3], gs.at[2, :, lanes_at(LANES + side * half, half)]),
-        copies.local(g_two, gs.at[2, :, lanes_at(LANES + other * half, half // 2)]),
+        copies.local(g_two, gs.at[2, :, lanes_at(LANES + other * half, half // 4)]),
     ]
     extra = ((g_own.at[:, own3:], side), (g_extra, other))
     extra_loads = [
@@ -969,7 +971,8 @@
     depth = conv_grad.shape[0] * chans
     part_loads = [copies.local(gw.at[:, i * depth : (i + 1) * depth], parts.at[i, :, :depth]) for i in (0, 1)]
     part_loads += [copies.local(gp.at[:, i * chans : (i + 1) * chans], parts.at[i, :, depth:]) for i in (0, 1)]
-    for copy in own_loads + loads + part_loads:
+    cot_loads = [copies.local(cin.at[w], cbuf.at[w]) for w in range(windows)]
+    for copy in own_loads + loads + part_loads + cot_loads:
         copy.start()
 
     @pl.when(group == 0)
@@ -979,8 +982,8 @@
 
     place.greet()
     t4 = copies.remote(
-        g_own.at[:, own2 + half // 2 : own3],
-        gs.at[2, :, lanes_at(LANES + side * half + half // 2, half // 2)],
+        g_own.at[:, own2 + half // 4 : own3],
+        gs.at[2, :, lanes_at(LANES + side * half + half // 4, half - half // 4)],
         partner,
     )
     t4_first = [
@@ -1138,7 +1141,6 @@
         copy.wait()
     halos["own"].finish()
     through(side)
-    keep(side)
     s_core.wait_recv()
     parts[:, core_rows(core), :] += parts_core[...]
     s_win.start()
@@ -1146,7 +1148,6 @@
     own_loads[2].wait()
     t4.wait_recv()
     halos["third"].start()
-    quarter_keep = copies.local(gs.at[3, :, 0:bins], grads.at[3])
 
     @pl.when(group == 0)
     def _():
@@ -1160,7 +1161,6 @@
 
     halos["third"].finish()
     through(2)
-    keep(2)
     s_win.wait_recv()
     parts[:, win_rows(place.win), :] += parts_win[...]
     for copy in s_z:
@@ -1170,7 +1170,6 @@
     def _():
         halos["quarter"].finish()
         through(3)
-        quarter_keep.start()
 
     for copy in s_z_in:
         copy.wait_recv()
@@ -1191,29 +1190,59 @@
     for copy in g_z:
         copy.start()
     through(other)
-    keep(other)
     plane = PlaneSum(copies, place, msg, slots)
     plane.start([to_row(acc1[...]), to_row(acc2[...])])
     for copy in g_z_in:
         copy.wait_recv()
     g_win.start()
-    rows_out[...] = plane.finish()
+    total = plane.finish()
+    rows_out[...] = total
+    mean, scale, filled, gain = (rows_in[i : i + 1, :] for i in (0, 1, 2, 6))
+    factor = gain * scale
+    slope = factor * scale * total[1:2, :] / filled
+    for at, row in enumerate((factor, slope, factor * total[0:1, :] / filled - mean * slope)):
+        cols[at] = to_column(row)
+    for copy in cot_loads:
+        copy.wait()
+
+    def last(slot):
+        window = order[slot]
+
+        def tile(i):
+            at = lanes_at(i * TILE, TILE)
+            mask = valid_lanes(place.shard * bins + i * TILE, TILE, order.size(slot)) > 0.0
+
+            def body(rows):
+                factor, slope, shift = (spread_lanes(cols[i, rows, :], TILE) for i in range(3))
+                back = factor * gs[slot, rows, at].astype(F32)
+                back = back - xbuf[window, rows, at].astype(F32) * slope - shift
+                sent = cbuf[window, rows, at].astype(F32)
+                gs[slot, rows, at] = (sent + jnp.where(mask, back, 0.0)).astype(BF16)
+
+            by_rows(chans, body)
+
+        times(bins // TILE, tile)
+
+    last(side)
+    keep(side)
     g_win_in.wait_recv()
     g_core.start()
-    plane.drain()
+    last(2)
+    keep(2)
     g_core_in.wait_recv()
     for tap in range(conv_grad.shape[0]):
         conv_grad[tap] = jnp.transpose(summed[:, tap * chans : (tap + 1) * chans])
     point_grad[...] = summed[:, depth:]
+    last(3)
+    keep(3)
+    last(other)
+    keep(other)
+    plane.drain()
     for copy in [s_core, s_win, s_side, *s_z, *g_z, g_win, g_core]:
         copy.wait_send()
     for copy in keeps:
         copy.wait()
 
-    @pl.when(group == 0)
-    def _():
-        quarter_keep.wait()
-
     @pl.when(group > 0)
     def _():
         for copy in e_home:
@@ -1226,9 +1255,9 @@
 
 
 def last_kernel(
-    lengths, x, c, act, grad, point, bias, rows_one, rows_two, conv_in, point_in,
+    lengths, x, act, grad, point, bias, rows_one, rows_two, conv_in, point_in,
     out, grad_out, gain_in, offset_in, gain_mid, offset_mid, grad_bias, conv_out, point_out,
-    weight, cols, tmp,
+    weight, more, tmp,
 ):
     window, tile = pl.program_id(0), pl.program_id(1)
     side, shard = lax.axis_index("ch"), lax.axis_index("seq")
@@ -1238,14 +1267,8 @@
     @pl.when((window == 0) & (tile == 0))
     def _():
         weight[...] = jnp.transpose(point[...])
-        mean, scale, filled, gain = (rows_one[i : i + 1, :] for i in (0, 1, 2, 6))
         beta, gamma = rows_two[0:1, :], rows_two[1:2, :]
-        factor = gain * scale
-        slope = factor * scale * gamma / filled
-        for at, row in enumerate(
-            (factor, slope, factor * beta / filled - mean * slope, bias[...].reshape(beta.shape))
-        ):
-            cols[at] = to_column(row)
+        more[...] = to_column(bias[...].reshape(beta.shape))
         size = gain_in.shape[0]
         gain_in[...] = gamma.reshape(size)
         offset_in[...] = beta.reshape(size)
@@ -1258,17 +1281,14 @@
     bins = pl.num_programs(1) * size
     mask = valid_lanes(shard * bins + tile * size, size, lengths[window]) > 0.0
     tmp[...] = dot(weight[...], act[0])
+    grad_out[...] = grad[...]
+
     def body(rows):
-        factor, slope, shift, more = (spread_lanes(cols[i, rows, :], TILE) for i in range(4))
+        added = spread_lanes(more[rows, :], TILE)
         for at in range(0, size, TILE):
             lanes = slice(at, at + TILE)
-            kept = mask[:, lanes]
-            xs = x[0, rows, lanes].astype(F32)
-            out[0, rows, lanes] = (xs + jnp.where(kept, tmp[rows, lanes], 0.0) + more).astype(BF16)
-            back = factor * grad[0, rows, lanes].astype(F32) - xs * slope - shift
-            grad_out[0, rows, lanes] = (
-                c[0, rows, lanes].astype(F32) + jnp.where(kept, back, 0.0)
-            ).astype(BF16)
+            kept = jnp.where(mask[:, lanes], tmp[rows, lanes], 0.0)
+            out[0, rows, lanes] = (x[0, rows, lanes].astype(F32) + kept + added).astype(BF16)
 
     by_rows(x.shape[1], body)
 
@@ -1301,7 +1321,7 @@
         out_shape=[
             shape((windows, bottle, bins), BF16),
             shape((bottle, packed), BF16),
-            shape((bottle, half // 2), BF16),
+            shape((bottle, half // 4), BF16),
             shape((bottle, eighth), BF16),
             shape((bottle, 2 * taps * chans), F32),
             shape((bottle, 2 * chans), F32),
@@ -1354,7 +1374,7 @@
     share = bottle // PLANE
     acts, grads, rows_two, conv_grad, point_grad = pl.pallas_call(
         second_kernel,
-        in_specs=[smem, hbm, hbm, hbm, hbm, hbm, hbm, hbm, vmem, vmem],
+        in_specs=[smem, hbm, hbm, hbm, hbm, hbm, hbm, hbm, hbm, vmem, vmem],
         out_specs=[hbm, hbm, vmem, vmem, vmem],
         out_shape=[
             shape((windows, bottle, bins), BF16),
@@ -1363,9 +1383,10 @@
             shape((taps, chans, bottle), F32),
             shape((bottle, chans), F32),
         ],
-        input_output_aliases={2: 0},
+        input_output_aliases={3: 0},
         scratch_shapes=[
             pltpu.VMEM((windows, bottle, bins + 2 * LANES), BF16),
+            pltpu.VMEM((windows, chans, bins), BF16),
             pltpu.VMEM((windows, chans, bins), BF16),
             pltpu.VMEM((windows, bottle, LANES), BF16),
             pltpu.VMEM((windows, bottle, LANES), BF16),
@@ -1390,7 +1411,7 @@
             collective_id=1, has_side_effects=True, vmem_limit_bytes=VMEM_BYTES
         ),
         cost_estimate=pl.CostEstimate(flops=60 * 10**9, bytes_accessed=10**8, transcendentals=0),
-    )(lengths, inputs, acts, g_own, g_two, g_extra, gw, gp, conv_weight, rows_one)
+    )(lengths, inputs, cotangent, acts, g_own, g_two, g_extra, gw, gp, conv_weight, rows_one)
 
     def slot_of(window, sizes):
         rank = jnp.int32(0)
@@ -1415,7 +1436,7 @@
             num_scalar_prefetch=1,
             grid=(windows, bins // tile),
             in_specs=[
-                at, at, at_slot, at_slot,
+                at, at_slot, at_slot,
                 whole(bottle, chans), line(chans), whole(8, chans), whole(8, chans), conv_at, point_at,
             ],
             out_specs=[
@@ -1424,7 +1445,7 @@
             ],
             scratch_shapes=[
                 pltpu.VMEM((chans, bottle), BF16),
-                pltpu.VMEM((4, chans, LANES), F32),
+                pltpu.VMEM((chans, LANES), F32),
                 pltpu.VMEM((chans, tile), F32),
             ],
         ),
@@ -1442,7 +1463,7 @@
         compiler_params=pltpu.CompilerParams(vmem_limit_bytes=VMEM_BYTES),
         cost_estimate=pl.CostEstimate(flops=4 * 10**9, bytes_accessed=6 * 10**7, transcendentals=0),
     )(
-        lengths, inputs, cotangent, acts, grads, point_weight, point_bias, rows_one, rows_two,
+        lengths, inputs, acts, grads, point_weight, point_bias, rows_one, rows_two,
         conv_grad, point_grad,
     )
     return (

time: 390 us -> 387 us (level)
    pallas_call x1, Pallas kernels: 125 us -> 132 us  [local_pair(): pl.pallas_call(second_kernel, in_specs=[smem, hbm, hbm, hbm, hbm, hbm, hb...]
    pallas_call x1, Pallas kernels: 26 us -> 21 us  [local_pair(): pl.pallas_call(last_kernel, grid_spec=pltpu.PrefetchScalarGridSpec(num_sc...]
    pallas_call x1, Pallas kernels: 237 us -> 233 us  [local_pair(): pl.pallas_call(first_kernel, in_specs=[smem, hbm, hbm, hbm, hbm, vmem, vm...]
where the time goes in v5:
time: 387 us
  Pallas kernels  386 us (100%)
    pallas_call x1, Pallas kernels, local_pair(): pl.pallas_call(first_kernel, in_specs=[smem, hbm, hbm, hbm, hbm, vmem, vm...  233 us
    pallas_call x1, Pallas kernels, local_pair(): pl.pallas_call(second_kernel, in_specs=[smem, hbm, hbm, hbm, hbm, hbm, hb...  132 us
    pallas_call x1, Pallas kernels, local_pair(): pl.pallas_call(last_kernel, grid_spec=pltpu.PrefetchScalarGridSpec(num_sc...  21 us

profile of v5, /device:TPU:0, one launch (start us, length us, event | category | flops | bytes accessed | tf_op | source)
XLA Modules:
  0.0 387.0 jit_solution(17843905655536440415)
XLA Ops:
  0.6 233.1 %shard_map.169 = (bf16[4,384,3072]{2,1,0:T(8,128)(2,1)}, bf16[384,4992]{1,0:T(8,128)(2,1)}, bf16[384,384]{1,0:T(8,128)(2,1)}, bf16[384,384]{1,0:T(8,128)(2,1)}, ...) custom-call(s32[4]{0:T(128)} %lengths.5, bf16[4,384,3072]{2,1,0:T(8,128)(2,1)} %x.1, ...), custom_call_target="tpu_custom_call" | custom-call | flops 60000002048 | bytes 100000000 | tf_op jit(solution)/shard_map/pallas_call | solution.py:1317
  233.7 132.1 %shard_map.170 = (bf16[4,384,3072]{2,1,0:T(8,128)(2,1)}, bf16[4,384,3072]{2,1,0:T(8,128)(2,1)}, f32[8,384]{1,0:T(8,128)}, f32[3,384,384]{2,1,0:T(8,128)}, f32[384,384]{1,0:T(8,128)}) custom-call(s32[4]{0:T(128)} %lengths.5, bf16[4,384,3072]{2,1,0:T(8,128)(2,1)} %x.1, bf16[4,384,3072]{2,1,0:T(8,128)(2,1)} %cin.3, ...), custom_call_target="tpu_custom_call", output_to_operand_aliasing={{0}: (3, {})} | custom-call | flops 60000002048 | bytes 100000000 | tf_op jit(solution)/shard_map/pallas_call | solution.py:1375
  365.8 21.0 %shard_map.171 = (bf16[4,384,3072]{2,1,0:T(8,128)(2,1)}, bf16[4,384,3072]{2,1,0:T(8,128)(2,1)}, f32[384]{0:T(512)}, f32[384]{0:T(512)}, f32[1,192]{1,0:T(1,128)}...) custom-call(s32[4]{0:T(128)} %lengths.5, bf16[4,384,3072]{2,1,0:T(8,128)(2,1)} %x.1, ...), custom_call_target="tpu_custom_call" | custom-call | flops 4000000000 | bytes 60000000 | tf_op jit(solution)/shard_map/pallas_call | solution.py:1433
